TPU v7x, 32 devices: a whole 2x2x4 slice. The times are simulated.
32 devices in a mesh: parts: 2 (over y), batch: 4 (over z), grp: 4 (over x, core).
Axes of the slice: x: 2, y: 2, z: 4, core: 2. Of those that a mesh axis runs over, the one named last changes fastest.
Arguments:
- queries: bfloat16 [8192, 2048], P(('parts', 'batch', 'grp')), parts along dimension 0, may hold values from -2 to 2
- passages: bfloat16 [4096, 2048], P(('parts', 'batch', 'grp')), parts along dimension 0, may hold values from -2 to 2
- hard_owners: int32 [8192, 2], P(('parts', 'batch', 'grp')), parts along dimension 0, may hold values from 0 to 3, all different within a row; in each aligned block of 256 rows (0 to 255, 256 to 511, ...) at most 170 rows name the same one
Outputs:
- query_loss: float32 [8192], P(('parts', 'batch', 'grp')), parts along dimension 0
- query_grad: bfloat16 [8192, 2048], P(('parts', 'batch', 'grp')), parts along dimension 0
- passage_grad: bfloat16 [4096, 2048], P(('parts', 'batch', 'grp')), parts along dimension 0
There are 2 independent parts, one for each index of `parts`. A program takes and returns all parts, laid end to end along the dimension named above; each array names one. Nothing has to cross between parts.
Inputs may be any that keep to these rules, and one draw needn't show every extreme that they name: `hard_owners`: each row names 2 different batch indices. Among the 256 rows of one device no index is named more than 170 times, and on some devices some index is named exactly 170 times.
All inputs are finite; a program needn't handle non-finite values.
Results may differ from a plain program's by a relative error of at most 0.012.
Values may be sent and summed in bfloat16 or wider, within the bound.
A program may use at most 128 MiB of HBM per device.

v0:
```python
import jax
import jax.numpy as jnp
from jax import lax
from jax.sharding import PartitionSpec as P

sharpness_factor = 20.0
norm_eps = 1e-06


def shortened(value):

    def short(part):
        return part.astype(jnp.bfloat16) if part.dtype == jnp.float32 else part

    return jax.tree.map(short, value)


def unit_rows(embedded):
    widened = embedded.astype(jnp.float32)
    inverse_norm = lax.rsqrt(jnp.sum(widened * widened, axis=1, keepdims=True) + norm_eps)
    return (widened * inverse_norm, inverse_norm)


def slot_layout(owner_table, owner_count, capacity):
    owner_list = owner_table.reshape(-1)
    onehot = (owner_list[:, None] == jnp.arange(owner_count, dtype=jnp.int32)[None, :]).astype(
        jnp.int32
    )
    before = jnp.cumsum(onehot, axis=0) - onehot
    rank_in_slot = jnp.sum(before * onehot, axis=1)
    slot_place = owner_list * capacity + rank_in_slot
    pair_query = jnp.arange(owner_list.shape[0], dtype=jnp.int32) // owner_table.shape[1]
    holder = (
        jnp.full((owner_count * capacity,), owner_table.shape[0], jnp.int32)
        .at[slot_place]
        .set(pair_query)
    )
    return (slot_place, holder)


def back_project(unit, inverse_norm, direction):
    inner = jnp.sum(unit * direction, axis=1, keepdims=True)
    return (inverse_norm * (direction - unit * inner)).astype(jnp.bfloat16)


def local(queries, passages, hard_owners):
    query_unit, query_norm = unit_rows(queries)
    passage_unit, passage_norm = unit_rows(passages)
    query_half = query_unit.astype(jnp.bfloat16)
    passage_half = passage_unit.astype(jnp.bfloat16)
    query_rows, embed_width = queries.shape
    passage_rows = passages.shape[0]
    picks_each = hard_owners.shape[1]
    batch_count = lax.axis_size("batch")
    group_count = lax.axis_size("grp")
    capacity = max(2, min(query_rows, 4 * query_rows * picks_each // (3 * batch_count)))
    slot_place, holder = slot_layout(hard_owners, batch_count, capacity)
    padded_queries = jnp.concatenate(
        [query_half, jnp.zeros((1, embed_width), jnp.bfloat16)], axis=0
    )
    outgoing = padded_queries[holder].reshape(batch_count, capacity, embed_width)
    arrived = lax.all_to_all(outgoing, "batch", split_axis=0, concat_axis=0, tiled=True).reshape(
        batch_count * capacity, embed_width
    )
    seat_similarity_values = sharpness_factor * jnp.einsum(
        "md,cd->mc", arrived, passage_half, preferred_element_type=jnp.float32
    )
    passage_wide = passage_half.astype(jnp.float32)
    document_vectors_by_team = lax.all_gather(passage_half, "grp", axis=0, tiled=True)
    entering_similarities = sharpness_factor * jnp.einsum(
        "id,jd->ij", query_half, document_vectors_by_team, preferred_element_type=jnp.float32
    )
    column = (
        lax.axis_index("grp") * passage_rows
        + jnp.arange(query_rows, dtype=jnp.int32) % passage_rows
    )
    matching_indicator = (
        jnp.arange(group_count * passage_rows, dtype=jnp.int32)[None, :] == column[:, None]
    )
    totals_in = jnp.sum(jnp.exp(entering_similarities), axis=1)
    returned = lax.all_to_all(
        seat_similarity_values.reshape(batch_count, capacity, passage_rows).astype(jnp.bfloat16),
        "batch",
        split_axis=0,
        concat_axis=0,
        tiled=True,
    ).astype(jnp.float32)
    pair_scores = returned.reshape(batch_count * capacity, passage_rows)[slot_place]
    totals = totals_in + jnp.sum(
        jnp.exp(pair_scores).reshape(query_rows, picks_each * passage_rows), axis=1
    )
    normalizer_logarithm = jnp.log(totals)
    pair_weights = jnp.exp(pair_scores - jnp.repeat(normalizer_logarithm, picks_each)[:, None])
    weight_slots = (
        jnp.zeros((batch_count * capacity, passage_rows), jnp.float32)
        .at[slot_place]
        .set(pair_weights)
    )
    slot_weights = (
        lax.all_to_all(
            weight_slots.reshape(batch_count, capacity, passage_rows).astype(jnp.bfloat16),
            "batch",
            split_axis=0,
            concat_axis=0,
            tiled=True,
        )
        .astype(jnp.float32)
        .reshape(batch_count * capacity, passage_rows)
    )
    seat_backward_derivative = sharpness_factor * jnp.dot(
        slot_weights, passage_wide, precision=lax.Precision.HIGHEST
    )
    home_rows = lax.all_to_all(
        shortened(seat_backward_derivative.reshape(batch_count, capacity, embed_width)),
        "batch",
        split_axis=0,
        concat_axis=0,
        tiled=True,
    )
    pair_rows = home_rows.reshape(batch_count * capacity, embed_width)[slot_place]
    hard_dir = jnp.sum(pair_rows.reshape(query_rows, picks_each, embed_width), axis=1)
    hard_negative_documents = sharpness_factor * jnp.einsum(
        "mc,md->cd", slot_weights.astype(jnp.bfloat16), arrived, preferred_element_type=jnp.float32
    )
    query_loss = normalizer_logarithm - jnp.sum(
        jnp.where(matching_indicator, entering_similarities, 0.0), axis=1
    )
    upstream_derivative = (
        sharpness_factor
        * (
            jnp.exp(entering_similarities - normalizer_logarithm[:, None])
            - matching_indicator.astype(jnp.float32)
        )
    ).astype(jnp.bfloat16)
    query_dir = (
        jnp.dot(upstream_derivative, document_vectors_by_team, preferred_element_type=jnp.float32)
        + hard_dir
    )
    passage_dir = (
        lax.psum_scatter(
            jnp.einsum(
                "ij,id->jd", upstream_derivative, query_half, preferred_element_type=jnp.float32
            ).astype(jnp.bfloat16),
            "grp",
            scatter_dimension=0,
            tiled=True,
        ).astype(jnp.float32)
        + hard_negative_documents
    )
    return (
        query_loss,
        back_project(query_unit, query_norm, query_dir),
        back_project(passage_unit, passage_norm, passage_dir),
    )


def solution(mesh):
    placed = (
        P(("parts", "batch", "grp"), None),
        P(("parts", "batch", "grp"), None),
        P(("parts", "batch", "grp"), None),
    )
    return jax.shard_map(
        local,
        mesh=mesh,
        in_specs=placed,
        out_specs=(
            P(("parts", "batch", "grp")),
            P(("parts", "batch", "grp"), None),
            P(("parts", "batch", "grp"), None),
        ),
        check_vma=False,
    )
```

profile of v0, /device:TPU:0, one launch (start us, length us, event | category | flops | bytes accessed | tf_op | source)
XLA Modules:
  0.0 239.3 jit_solution(8851199911801772278)
XLA Ops:
  7.2 0.9 copy.7
  8.1 0.1 eq.44
  8.2 0.1 eq.40
  8.4 0.7 broadcast_multiply_fusion
  9.1 1.2 reduce-window.6
  10.3 0.2 slice_reduce_fusion
  10.5 0.2 reduce-window.9
  10.8 0.1 copy.6
  10.9 0.1 mul.111
  11.1 2.4 %scatter_custom_fusion = s32[680]{0:T(1024)S(1)} fusion(s32[512]{0:T(512)S(1)} %bitcast.37, s32[512]{0:T(512)S(1)} %add_select_fusion, s32[]{:T(128)} %constant.54.clone.1), kind=kCustom, calls=%fused_computation.63 | custom fusion | bytes 2724 | tf_op jit(solution)/shard_map/scatter | solution.py:36
  13.6 1.5 fusion.9
  15.1 0.2 fusion.2
  15.4 0.1 concatenate.3
  15.5 4.2 %gather_fusion = bf16[680,2048]{1,0:T(8,128)(2,1)} fusion(bf16[257,2048]{1,0:T(8,128)(2,1)S(1)} %concatenate.3, s32[1024]{0:T(1024)S(1)} %pad_clamp_fusion.1), kind=kCustom, calls=%fused_computation | custom fusion | bytes 5573280 | tf_op jit(solution)/shard_map/gather | solution.py:61
  19.6 4.1 %reshape.115 = bf16[4,170,2048]{2,1,0:T(8,128)(2,1)} reshape(bf16[680,2048]{1,0:T(8,128)(2,1)} %gather_fusion) | data formatting | bytes 5570560 | tf_op jit(solution)/shard_map/reshape | solution.py:61
  23.7 6.4 %all-to-all-start = ((bf16[4,170,2048]{2,1,0:T(8,128)(2,1)}), bf16[4,170,2048]{2,1,0:T(8,128)(2,1)S(1)}, u32[]{:S(2)}, u32[]{:S(2)}) async-start(bf16[4,170,2048]{2,1,0:T(8,128)(2,1)} %reshape.115), calls=%async_computation | async-start | bytes 5767168 | tf_op jit(solution)/shard_map/all_to_all | solution.py:62
  30.2 0.2 fusion.18
  30.4 0.9 fusion.12
  31.4 63.8 %all-to-all-done = bf16[4,170,2048]{2,1,0:T(8,128)(2,1)S(1)} async-done(((bf16[4,170,2048]{2,1,0:T(8,128)(2,1)}), bf16[4,170,2048]{2,1,0:T(8,128)(2,1)S(1)}, u32[]{:S(2)}, u32[]{:S(2)}) %all-to-all-start) | async-done | bytes 2785312 | tf_op jit(solution)/shard_map/all_to_all | solution.py:62
  95.2 2.3 reshape.116
  97.5 3.3 %fusion.13 = bf16[680,128]{1,0:T(8,128)(2,1)} fusion(bf16[680,2048]{1,0:T(8,128)(2,1)} %reshape.116, bf16[128,2048]{1,0:T(8,128)(2,1)S(1)} %copy-done.5), kind=kOutput, calls=%fused_computation.28 | convolution fusion | flops 356689920 | bytes 3483648 | tf_op jit(solution)/shard_map/md,cd->mc/dot_general | solution.py:65
  100.9 1.6 convert_element_type.72
  102.5 3.4 %all-to-all-start.1 = ((bf16[4,170,128]{2,1,0:T(8,128)(2,1)}), bf16[4,170,128]{2,1,0:T(8,128)(2,1)S(1)}, u32[]{:S(2)}, u32[]{:S(2)}) async-start(bf16[4,170,128]{2,1,0:T(8,128)(2,1)} %convert_element_type.72), calls=%async_computation.1 | async-start | bytes 360448 | tf_op jit(solution)/shard_map/all_to_all | solution.py:81
  106.0 3.5 %select_reduce_fusion = (f32[256]{0:T(256)S(1)}, f32[256]{0:T(256)S(1)}, f32[256,512]{1,0:T(8,128)}) fusion(s32[256]{0:T(256)S(1)} %fusion.33, bf16[256,2048]{1,0:T(8,128)(2,1)} %copy-done.2, bf16[512,2048]{1,0:T(8,128)(2,1)} %all-gather.2.cloned.1.call-done), kind=kOutput, calls=%fused_computation.35 | convolution fusion | flops 537525760 | bytes 3673088 | tf_op jit(solution)/shard_map/id,jd->ij/dot_general | solution.py:70
  109.5 2.9 %all-to-all-done.1 = bf16[4,170,128]{2,1,0:T(8,128)(2,1)S(1)} async-done(((bf16[4,170,128]{2,1,0:T(8,128)(2,1)}), bf16[4,170,128]{2,1,0:T(8,128)(2,1)S(1)}, u32[]{:S(2)}, u32[]{:S(2)}) %all-to-all-start.1) | async-done | bytes 174112 | tf_op jit(solution)/shard_map/all_to_all | solution.py:81
  112.5 1.0 gather_fusion.1
  113.5 0.2 exponential_reduce_fusion.1
  113.7 0.1 reduce_sum.99
  113.9 0.6 fusion.34
  114.5 3.7 %convolution_convert_fusion = bf16[512,2048]{1,0:T(8,128)(2,1)} fusion(bf16[256,2048]{1,0:T(8,128)(2,1)} %copy-done.2, f32[256,512]{1,0:T(8,128)} %get-tuple-element.7, f32[256]{0:T(256)S(1)} %get-tuple-element.6, s32[256]{0:T(256)S(1)} %fusion.33), kind=kOutput, calls=%fused_computation.6 | convolution fusion | flops 538705920 | bytes 3672064 | tf_op jit(solution)/shard_map/ij,id->jd/dot_general | solution.py:141
  118.3 0.1 sub.45
  118.5 2.9 %scatter_custom_fusion.1 = f32[680,128]{1,0:T(8,128)} fusion(s32[512]{0:T(512)} %bitcast.39, f32[512,128]{1,0:T(8,128)} %copy-done.7, f32[]{:T(128)} %constant.27.clone.1, f32[512]{0:T(512)S(1)} %sub.45), kind=kCustom, calls=%fused_computation.38 | custom fusion | flops 65536 | bytes 612864 | tf_op jit(solution)/shard_map/scatter | solution.py:97
  121.4 1.7 convert_element_type.75
  123.1 1.6 convert_element_type.76
  124.7 10.8 %all_to_all.20 = bf16[4,170,128]{2,1,0:T(8,128)(2,1)} all-to-all(bf16[4,170,128]{2,1,0:T(8,128)(2,1)} %convert_element_type.76), channel_id=1, replica_groups=mesh['parts'=2,'batch'=4,'grp'=4] {'batch'}, dimensions={0} | all-to-all | bytes 348160 | tf_op jit(solution)/shard_map/all_to_all | solution.py:100
  135.5 1.6 reshape.119
  137.2 3.4 %multiply_convert_fusion = bf16[680,2048]{1,0:T(8,128)(2,1)} fusion(bf16[680,128]{1,0:T(8,128)(2,1)} %reshape.119, bf16[128,2048]{1,0:T(8,128)(2,1)S(1)} %copy-done.6), kind=kOutput, calls=%fused_computation.5 | convolution fusion | flops 359301120 | bytes 3483648 | tf_op jit(solution)/shard_map/dot_general | solution.py:110
  140.6 4.1 %convert_element_type.78 = bf16[4,170,2048]{2,1,0:T(8,128)(2,1)} reshape(bf16[680,2048]{1,0:T(8,128)(2,1)} %multiply_convert_fusion) | data formatting | bytes 5570560 | tf_op jit(solution)/shard_map/convert_element_type | solution.py:13
  144.7 4.7 %all-to-all-start.3 = ((bf16[4,170,2048]{2,1,0:T(8,128)(2,1)}), bf16[4,170,2048]{2,1,0:T(8,128)(2,1)}, u32[]{:S(2)}, u32[]{:S(2)}) async-start(bf16[4,170,2048]{2,1,0:T(8,128)(2,1)} %convert_element_type.78), calls=%async_computation.3 | async-start | bytes 5767168 | tf_op jit(solution)/shard_map/all_to_all | solution.py:113
  149.5 1.9 fusion.14
  151.4 1.1 fusion.17
  152.5 58.8 %all-to-all-done.3 = bf16[4,170,2048]{2,1,0:T(8,128)(2,1)} async-done(((bf16[4,170,2048]{2,1,0:T(8,128)(2,1)}), bf16[4,170,2048]{2,1,0:T(8,128)(2,1)}, u32[]{:S(2)}, u32[]{:S(2)}) %all-to-all-start.3) | async-done | bytes 2785312 | tf_op jit(solution)/shard_map/all_to_all | solution.py:113
  211.3 2.6 %reshape.120 = bf16[680,2048]{1,0:T(8,128)(2,1)S(1)} reshape(bf16[4,170,2048]{2,1,0:T(8,128)(2,1)} %all-to-all-done.3) | data formatting | bytes 5570560 | tf_op jit(solution)/shard_map/reshape | solution.py:120
  213.9 3.3 %gather_fusion.2 = bf16[512,2048]{1,0:T(8,128)(2,1)} fusion(bf16[680,2048]{1,0:T(8,128)(2,1)S(1)} %reshape.120, s32[1024]{0:T(1024)S(1)} %pad_clamp_fusion), kind=kCustom, calls=%fused_computation.2 | custom fusion | bytes 4196352 | tf_op jit(solution)/shard_map/gather | solution.py:120
  217.2 4.4 %reshape.121 = bf16[256,2,2048]{2,1,0:T(2,128)(2,1)} reshape(bf16[512,2048]{1,0:T(8,128)(2,1)} %gather_fusion.2) | data formatting | bytes 4194304 | tf_op jit(solution)/shard_map/reshape | solution.py:121
  221.6 6.8 %reduce_sum.102 = bf16[256,2048]{1,0:T(8,128)(2,1)S(1)} reduce(bf16[256,2,2048]{2,1,0:T(2,128)(2,1)} %reshape.121, bf16[]{:T(256)} %constant.53.clone.1), dimensions={1}, to_apply=%region_11.12 | reduce | flops 524288 | bytes 3145730 | tf_op jit(solution)/shard_map/reduce_sum | solution.py:121
  228.4 2.6 %fusion.5 = (f32[256]{0:T(256)S(1)}, f32[256,2048]{1,0:T(8,128)S(1)}) fusion(bf16[256,2048]{1,0:T(8,128)(2,1)S(1)} %copy-done.1, f32[256]{0:T(256)S(1)} %add_rsqrt_fusion, bf16[256,2048]{1,0:T(8,128)(2,1)S(1)} %reduce_sum.102, bf16[512,2048]{1,0:T(8,128)(2,1)} %all-gather.2.cloned.1.call-done, f32[256,512]{1,0:T(8,128)S(1)} %copy-done.8, ...), kind=kOutput, calls=%fused_computation.16 | convolution fusion | flops 540802816 | bytes 6819840 | tf_op jit(solution)/shard_map/dot_general | solution.py:136
  231.0 1.4 fusion.8
  (48 shorter events, 0.6 us)
Async XLA Ops:
  7.2 7.9 %copy-start = (bf16[256,2048]{1,0:T(8,128)(2,1)S(1)}, bf16[256,2048]{1,0:T(8,128)(2,1)}, u32[]{:S(2)}) copy-start(bf16[256,2048]{1,0:T(8,128)(2,1)} %param.3) | copy-start | bytes 3145732
  11.1 20.3 %copy-start.9 = (s32[512,1]{0,1:T(1,128)}, s32[512,1]{0,1:T(1,128)S(1)}, u32[]{:S(2)}) copy-start(s32[512,1]{0,1:T(1,128)S(1)} %compare_select_fusion) | copy-start | bytes 6148
  15.4 4.3 %copy-start.2 = (bf16[256,2048]{1,0:T(8,128)(2,1)}, bf16[256,2048]{1,0:T(8,128)(2,1)S(1)}, u32[]{:S(2)}) copy-start(bf16[256,2048]{1,0:T(8,128)(2,1)S(1)} %fusion.2) | copy-start | bytes 3145732
  23.7 6.5 %copy-start.3 = (bf16[128,2048]{1,0:T(8,128)(2,1)S(1)}, bf16[128,2048]{1,0:T(8,128)(2,1)}, u32[]{:S(2)}) copy-start(bf16[128,2048]{1,0:T(8,128)(2,1)} %param.4) | copy-start | bytes 1572868
  23.7 71.5 %all-to-all-start = ((bf16[4,170,2048]{2,1,0:T(8,128)(2,1)}), bf16[4,170,2048]{2,1,0:T(8,128)(2,1)S(1)}, u32[]{:S(2)}, u32[]{:S(2)}) async-start(bf16[4,170,2048]{2,1,0:T(8,128)(2,1)} %reshape.115), calls=%async_computation | async-start | bytes 5767168 | tf_op jit(solution)/shard_map/all_to_all | solution.py:62
  30.2 75.8 %all-gather.2.cloned.1.call-start = ((), (), s32[]{:S(2)}) async-start(), calls=%async_computation.5 | async-start | bytes 2621440 | tf_op jit(solution)/shard_map/all_gather | solution.py:69
  30.4 67.1 %copy-start.10 = (f32[128]{0:T(128)}, f32[128]{0:T(128)S(1)}, u32[]{:S(2)}) copy-start(f32[128]{0:T(128)S(1)} %add_rsqrt_fusion.1) | copy-start | bytes 1540
  31.4 83.1 %copy-start.12 = (s32[256]{0:T(256)}, s32[256]{0:T(256)S(1)}, u32[]{:S(2)}) copy-start(s32[256]{0:T(256)S(1)} %fusion.33) | copy-start | bytes 3076
  31.4 66.1 %copy-start.5 = (bf16[128,2048]{1,0:T(8,128)(2,1)S(1)}, bf16[128,2048]{1,0:T(8,128)(2,1)}, u32[]{:S(2)}) copy-start(bf16[128,2048]{1,0:T(8,128)(2,1)} %fusion.12) | copy-start | bytes 1572868
  102.5 9.9 %all-to-all-start.1 = ((bf16[4,170,128]{2,1,0:T(8,128)(2,1)}), bf16[4,170,128]{2,1,0:T(8,128)(2,1)S(1)}, u32[]{:S(2)}, u32[]{:S(2)}) async-start(bf16[4,170,128]{2,1,0:T(8,128)(2,1)} %convert_element_type.72), calls=%async_computation.1 | async-start | bytes 360448 | tf_op jit(solution)/shard_map/all_to_all | solution.py:81
  105.9 43.5 %reduce-scatter.2.cloned.1.call-start = ((), (), s32[]{:S(2)}) async-start(), calls=%async_computation.6 | async-start | bytes 2621440 | tf_op jit(solution)/shard_map/reduce_scatter | solution.py:140
  113.5 4.7 %copy-start.7 = (f32[512,128]{1,0:T(8,128)}, f32[512,128]{1,0:T(8,128)S(1)}, u32[]{:S(2)}) copy-start(f32[512,128]{1,0:T(8,128)S(1)} %gather_fusion.1) | copy-start | bytes 786436
  118.2 19.0 %copy-start.6 = (bf16[128,2048]{1,0:T(8,128)(2,1)S(1)}, bf16[128,2048]{1,0:T(8,128)(2,1)}, u32[]{:S(2)}) copy-start(bf16[128,2048]{1,0:T(8,128)(2,1)} %fusion.12) | copy-start | bytes 1572868
  144.7 4.8 %copy-start.4 = (bf16[128,2048]{1,0:T(8,128)(2,1)S(1)}, bf16[128,2048]{1,0:T(8,128)(2,1)}, u32[]{:S(2)}) copy-start(bf16[128,2048]{1,0:T(8,128)(2,1)} %param.4) | copy-start | bytes 1572868
  144.7 4.8 %copy-start.11 = (f32[128]{0:T(128)S(1)}, f32[128]{0:T(128)}, u32[]{:S(2)}) copy-start(f32[128]{0:T(128)} %copy-done.10) | copy-start | bytes 1540
  144.7 66.6 %all-to-all-start.3 = ((bf16[4,170,2048]{2,1,0:T(8,128)(2,1)}), bf16[4,170,2048]{2,1,0:T(8,128)(2,1)}, u32[]{:S(2)}, u32[]{:S(2)}) async-start(bf16[4,170,2048]{2,1,0:T(8,128)(2,1)} %convert_element_type.78), calls=%async_computation.3 | async-start | bytes 5767168 | tf_op jit(solution)/shard_map/all_to_all | solution.py:113
  221.6 6.8 %copy-start.1 = (bf16[256,2048]{1,0:T(8,128)(2,1)S(1)}, bf16[256,2048]{1,0:T(8,128)(2,1)}, u32[]{:S(2)}) copy-start(bf16[256,2048]{1,0:T(8,128)(2,1)} %param.3) | copy-start | bytes 3145732
  221.6 6.8 %copy-start.8 = (f32[256,512]{1,0:T(8,128)S(1)}, f32[256,512]{1,0:T(8,128)}, u32[]{:S(2)}) copy-start(f32[256,512]{1,0:T(8,128)} %get-tuple-element.7) | copy-start | bytes 1572868
  221.6 6.8 %copy-start.13 = (s32[256]{0:T(256)S(1)}, s32[256]{0:T(256)}, u32[]{:S(2)}) copy-start(s32[256]{0:T(256)} %copy-done.12) | copy-start | bytes 3076
Sparse Core Ops, SparseCore 0:
  33.1 24.0 all-gather.1
  118.4 30.5 reduce-scatter.1
where the time goes:
time: 240 us; the launch traced here: 239 us
  waiting for transfers between devices  126 us (52%)
  local copies, waits for them, and re-layouts  35.6 us (15%)
  other arithmetic  19.9 us (8%)
  matrix products  18.5 us (8%)
  starting transfers between devices  14.6 us (6%)
  between operations  14.3 us (6%)
  blocking collectives  10.8 us (4%)
    all_to_all x1, waiting for transfers between devices, local(): lax.all_to_all(outgoing, 'batch', split_axis=0, concat_axis=0, tiled=True)  63.8 us
    all_to_all x1, waiting for transfers between devices, local(): lax.all_to_all(shortened(seat_backward_derivative.reshape(batch_count, ca...  58.8 us
    all_to_all x1, blocking collectives, local(): lax.all_to_all(weight_slots.reshape(batch_count, capacity, passage_rows)....  10.8 us
    reduce_sum x1, other arithmetic, local(): jnp.sum(pair_rows.reshape(query_rows, picks_each, embed_width), axis=1)  6.78 us
    all_to_all x1, starting transfers between devices, local(): lax.all_to_all(outgoing, 'batch', split_axis=0, concat_axis=0, tiled=True)  6.45 us
  transfers between devices with their start and end apart: 5, of which 3 were waited for; matrix products, arithmetic and copies ran while one was open for 13% of the time, Pallas kernels for 0%

commit v1 on v0

--- a/solution.py
+++ b/solution.py
@@ -43,7 +43,7 @@
     return (inverse_norm * (direction - unit * inner)).astype(jnp.bfloat16)
 
 
-def local(queries, passages, hard_owners):
+def local_slots(queries, passages, hard_owners):
     query_unit, query_norm = unit_rows(queries)
     passage_unit, passage_norm = unit_rows(passages)
     query_half = query_unit.astype(jnp.bfloat16)
@@ -154,6 +154,66 @@
     )
 
 
+def local_dense(queries, passages, hard_owners):
+    query_unit, query_norm = unit_rows(queries)
+    passage_unit, passage_norm = unit_rows(passages)
+    query_half = query_unit.astype(jnp.bfloat16)
+    passage_half = passage_unit.astype(jnp.bfloat16)
+    query_rows = queries.shape[0]
+    passage_rows = passages.shape[0]
+    batch_count = lax.axis_size("batch")
+    group_count = lax.axis_size("grp")
+    group_blocks = lax.all_gather(passage_half, "grp", axis=0, tiled=True)
+    line_blocks = lax.all_gather(passage_half, "batch", axis=0, tiled=True)
+    scores_in = sharpness_factor * jnp.einsum(
+        "id,jd->ij", query_half, group_blocks, preferred_element_type=jnp.float32
+    )
+    scores_hard = sharpness_factor * jnp.einsum(
+        "id,jd->ij", query_half, line_blocks, preferred_element_type=jnp.float32
+    )
+    block = jnp.arange(batch_count * passage_rows, dtype=jnp.int32)[None, :] // passage_rows
+    named = jnp.any(hard_owners[:, :, None] == block[:, None, :], axis=1)
+    column = (
+        lax.axis_index("grp") * passage_rows
+        + jnp.arange(query_rows, dtype=jnp.int32) % passage_rows
+    )
+    positive = (
+        jnp.arange(group_count * passage_rows, dtype=jnp.int32)[None, :] == column[:, None]
+    )
+    raised_in = jnp.exp(scores_in)
+    raised_hard = jnp.where(named, jnp.exp(scores_hard), 0.0)
+    totals = jnp.sum(raised_in, axis=1) + jnp.sum(raised_hard, axis=1)
+    log_total = jnp.log(totals)
+    query_loss = log_total - jnp.sum(jnp.where(positive, scores_in, 0.0), axis=1)
+    scale = sharpness_factor / totals
+    grad_in = (
+        raised_in * scale[:, None] - jnp.where(positive, sharpness_factor, 0.0)
+    ).astype(jnp.bfloat16)
+    grad_hard = (raised_hard * scale[:, None]).astype(jnp.bfloat16)
+    query_dir = jnp.dot(
+        grad_in, group_blocks, preferred_element_type=jnp.float32
+    ) + jnp.dot(grad_hard, line_blocks, preferred_element_type=jnp.float32)
+
+    def summed(grad, axis):
+        partial = jnp.einsum("ij,id->jd", grad, query_half, preferred_element_type=jnp.float32)
+        return lax.psum_scatter(
+            partial.astype(jnp.bfloat16), axis, scatter_dimension=0, tiled=True
+        ).astype(jnp.float32)
+
+    passage_dir = summed(grad_in, "grp") + summed(grad_hard, "batch")
+    return (
+        query_loss,
+        back_project(query_unit, query_norm, query_dir),
+        back_project(passage_unit, passage_norm, passage_dir),
+    )
+
+
+def local(queries, passages, hard_owners):
+    if lax.axis_size("batch") <= 8:
+        return local_dense(queries, passages, hard_owners)
+    return local_slots(queries, passages, hard_owners)
+
+
 def solution(mesh):
     placed = (
         P(("parts", "batch", "grp"), None),

time: 240 us -> 177 us (0.74)
  local copies, waits for them, and re-layouts: 35.6 us -> 0.02 us
  starting transfers between devices: 14.6 us -> 0.16 us
  waiting for transfers between devices: 126 us -> 140 us
  blocking collectives: 10.8 us -> 0 us
  other arithmetic: 19.9 us -> 9.69 us
  matrix products: 18.5 us -> 12.9 us
    all_to_all x3 -> x0, waiting for transfers between devices: 126 us -> none  [the longest x1 63.8 us: local(): lax.all_to_all(outgoing, 'batch', split_axis=0, concat_axis=0, tiled=True)]
    reduce_scatter x1 -> x2, waiting for transfers between devices: 0.02 us -> 70.5 us  [summed(): lax.psum_scatter(partial.astype(jnp.bfloat16), axis, scatter_dimension=0,...]
    all_gather x1 -> x2, waiting for transfers between devices: 0.02 us -> 68.5 us  [the longest x1 47.5 us: local_dense(): line_blocks = lax.all_gather(passage_half, 'batch', axis=0, tiled=True)]
    reshape x6 -> x0, local copies, waits for them, and re-layouts: 15 us -> none  [the longest x1 4.41 us: local(): pair_rows.reshape(query_rows, picks_each, embed_width)]
    all_to_all x3 -> x0, starting transfers between devices: 14.5 us -> none  [the longest x1 6.45 us: local(): lax.all_to_all(outgoing, 'batch', split_axis=0, concat_axis=0, tiled=True)]
    all_to_all x1 -> x0, blocking collectives: 10.8 us -> none  [local(): lax.all_to_all(weight_slots.reshape(batch_count, capacity, passage_rows)....]
    gather x3 -> x0, local copies, waits for them, and re-layouts: 8.54 us -> none  [the longest x1 4.15 us: local(): padded_queries[holder].reshape(batch_count, capacity, embed_width)]
    convert_element_type x3 -> x0, local copies, waits for them, and re-layouts: 7.38 us -> none  [the longest x1 4.1 us: short(): return part.astype(jnp.bfloat16) if part.dtype == jnp.float32 else part]
  transfers between devices with their start and end apart: 5 -> 4, of which waited for: 3 -> 4; matrix products, arithmetic and copies ran while one was open for 13% -> 6% of each run, Pallas kernels for 0% -> 0%
where the time goes in v1:
time: 177 us; the launch traced here: 176 us
  waiting for transfers between devices  140 us (79%)
  between operations  13.9 us (8%)
  matrix products  12.9 us (7%)
  other arithmetic  9.69 us (5%)
    reduce_scatter x2, waiting for transfers between devices, summed(): lax.psum_scatter(partial.astype(jnp.bfloat16), axis, scatter_dimension=0,...  70.5 us
    all_gather x1, waiting for transfers between devices, local_dense(): line_blocks = lax.all_gather(passage_half, 'batch', axis=0, tiled=True)  47.5 us
    all_gather x1, waiting for transfers between devices, local_dense(): group_blocks = lax.all_gather(passage_half, 'grp', axis=0, tiled=True)  21 us
    dot_general x2, matrix products, summed(): jnp.einsum('ij,id->jd', grad, query_half, preferred_element_type=jnp.floa...  4.41 us
    convert_element_type x2, other arithmetic, back_project(): return (inverse_norm * (direction - unit * inner)).astype(jnp.bfloat16)  3.81 us
  transfers between devices with their start and end apart: 4, of which 4 were waited for; matrix products, arithmetic and copies ran while one was open for 6% of the time, Pallas kernels for 0%

profile of v1, /device:TPU:0, one launch (start us, length us, event | category | flops | bytes accessed | tf_op | source)
XLA Modules:
  0.0 176.3 jit_solution(912268066409569081)
XLA Ops:
  7.2 0.0 copy-start.3
  7.2 0.0 copy-start
  7.2 0.0 all-gather.5.cloned.1.call-start
  7.2 1.3 fusion.17
  8.5 2.0 %fusion.10 = bf16[128,2048]{1,0:T(8,128)(2,1)} fusion(bf16[128,2048]{1,0:T(8,128)(2,1)} %param.4, f32[128]{0:T(128)S(1)} %add_rsqrt_fusion.1), kind=kLoop, calls=%fused_computation.17 | loop fusion | flops 786432 | bytes 1049088 | tf_op jit(solution)/shard_map/convert_element_type | solution.py:161
  10.5 0.0 all-gather.5.cloned.1.call-update
  10.6 0.0 all-gather.3.cloned.1.call-start
  10.6 0.7 all-gather.3.cloned.1.call-update
  11.3 0.0 reduce-scatter.3.cloned.1.call-start
  11.4 0.0 copy-done.3
  11.4 0.2 compare_reduce_fusion
  11.6 0.0 copy-done
  11.6 0.3 fusion.7
  11.9 47.5 %all-gather.5.cloned.1.call-done = bf16[512,2048]{1,0:T(8,128)(2,1)} async-done(((bf16[128,2048]{1,0:T(8,128)(2,1)}), bf16[512,2048]{1,0:T(8,128)(2,1)}) %all-gather.5.cloned.1.call-update) | async-done | bytes 2097168 | tf_op jit(solution)/shard_map/all_gather | solution.py:167
  59.4 2.5 %fusion.27 = (f32[256]{0:T(256)S(1)}, f32[256,512]{1,0:T(8,128)S(1)}) fusion(pred[256,512]{1,0:T(8,128)(4,1)S(1)} %compare_reduce_fusion, bf16[512,2048]{1,0:T(8,128)(2,1)} %all-gather.5.cloned.1.call-done, bf16[256,2048]{1,0:T(8,128)(2,1)S(1)} %copy-done, f32[256]{0:T(256)S(1)} %add_rsqrt_fusion), kind=kOutput, calls=%fused_computation.48 | convolution fusion | flops 538836736 | bytes 3803136 | tf_op jit(solution)/shard_map/id,jd->ij/dot_general | solution.py:171
  61.8 21.0 %all-gather.3.cloned.1.call-done = bf16[512,2048]{1,0:T(8,128)(2,1)} async-done(((bf16[128,2048]{1,0:T(8,128)(2,1)}), bf16[512,2048]{1,0:T(8,128)(2,1)}) %all-gather.3.cloned.1.call-update) | async-done | bytes 2097168 | tf_op jit(solution)/shard_map/all_gather | solution.py:166
  82.8 2.5 %exponential_reduce_fusion = (f32[256]{0:T(256)S(1)}, f32[256]{0:T(256)S(1)}, f32[256,512]{1,0:T(8,128)S(1)}) fusion(s32[256]{0:T(256)S(1)} %fusion.21, bf16[512,2048]{1,0:T(8,128)(2,1)} %all-gather.3.cloned.1.call-done, bf16[256,2048]{1,0:T(8,128)(2,1)S(1)} %copy-done, f32[256]{0:T(256)S(1)} %add_rsqrt_fusion), kind=kOutput, calls=%fused_computation.33 | convolution fusion | flops 539098624 | bytes 3674112 | tf_op jit(solution)/shard_map/id,jd->ij/dot_general | solution.py:168
  85.3 0.6 broadcast_divide_fusion
  85.9 2.2 %convolution_convert_fusion.1 = bf16[512,2048]{1,0:T(8,128)(2,1)} fusion(f32[256,512]{1,0:T(8,128)S(1)} %get-tuple-element.7, f32[256]{0:T(256)S(1)} %get-tuple-element.5, s32[256]{0:T(256)S(1)} %fusion.21, bf16[256,2048]{1,0:T(8,128)(2,1)S(1)} %copy-done, f32[256]{0:T(256)S(1)} %add_rsqrt_fusion), kind=kOutput, calls=%fused_computation.1 | convolution fusion | flops 540147712 | bytes 3673088 | tf_op jit(solution)/shard_map/ij,id->jd/dot_general | solution.py:198
  88.1 0.0 reduce-scatter.3.cloned.1.call-update
  88.1 0.0 reduce-scatter.5.cloned.1.call-start
  88.2 2.2 %convolution_convert_fusion = bf16[512,2048]{1,0:T(8,128)(2,1)} fusion(f32[256,512]{1,0:T(8,128)S(1)} %get-tuple-element.9, f32[256]{0:T(256)S(1)} %get-tuple-element.5, bf16[256,2048]{1,0:T(8,128)(2,1)S(1)} %copy-done, f32[256]{0:T(256)S(1)} %add_rsqrt_fusion), kind=kOutput, calls=%fused_computation | convolution fusion | flops 539754496 | bytes 3672064 | tf_op jit(solution)/shard_map/ij,id->jd/dot_general | solution.py:198
  90.4 0.0 reduce-scatter.5.cloned.1.call-update
  90.4 0.0 copy-start.2
  90.4 2.5 %fusion.22 = f32[256,2048]{1,0:T(8,128)S(1)} fusion(bf16[512,2048]{1,0:T(8,128)(2,1)} %all-gather.3.cloned.1.call-done, f32[256,512]{1,0:T(8,128)S(1)} %get-tuple-element.7, f32[256]{0:T(256)S(1)} %get-tuple-element.5, s32[256]{0:T(256)S(1)} %fusion.21), kind=kOutput, calls=%fused_computation.47 | convolution fusion | flops 537526272 | bytes 4720640 | tf_op jit(solution)/shard_map/dot_general | solution.py:193
  93.0 0.0 copy-done.2
  93.0 1.0 fusion.3
  94.0 0.0 copy-start.1
  94.0 1.4 fusion.6
  95.4 24.3 %reduce-scatter.3.cloned.1.call-done = bf16[128,2048]{1,0:T(8,128)(2,1)} async-done(((bf16[512,2048]{1,0:T(8,128)(2,1)}), bf16[128,2048]{1,0:T(8,128)(2,1)}) %reduce-scatter.3.cloned.1.call-update) | async-done | bytes 524304 | tf_op jit(solution)/shard_map/reduce_scatter | solution.py:199
  119.7 46.2 %reduce-scatter.5.cloned.1.call-done = bf16[128,2048]{1,0:T(8,128)(2,1)} async-done(((bf16[512,2048]{1,0:T(8,128)(2,1)}), bf16[128,2048]{1,0:T(8,128)(2,1)}) %reduce-scatter.5.cloned.1.call-update) | async-done | bytes 524304 | tf_op jit(solution)/shard_map/reduce_scatter | solution.py:199
  165.9 0.0 copy-done.1
  165.9 1.5 fusion.13
  167.4 2.4 %fusion.16 = bf16[128,2048]{1,0:T(8,128)(2,1)} fusion(bf16[128,2048]{1,0:T(8,128)(2,1)S(1)} %copy-done.1, bf16[128,2048]{1,0:T(8,128)(2,1)} %reduce-scatter.5.cloned.1.call-done, bf16[128,2048]{1,0:T(8,128)(2,1)} %reduce-scatter.3.cloned.1.call-done, f32[128]{0:T(128)S(1)} %fusion.13, f32[128]{0:T(128)S(1)} %add_rsqrt_fusion.1), kind=kLoop, calls=%fused_computation.25 | loop fusion | flops 2359296 | bytes 2098176 | tf_op jit(solution)/shard_map/convert_element_type | solution.py:43
  (4 shorter events, 0.0 us)
Async XLA Ops:
  7.2 4.2 %copy-start.3 = (s32[256,2]{0,1:T(2,128)S(1)}, s32[256,2]{0,1:T(2,128)}, u32[]{:S(2)}) copy-start(s32[256,2]{0,1:T(2,128)} %param.5) | copy-start | bytes 6148
  7.2 4.4 %copy-start = (bf16[256,2048]{1,0:T(8,128)(2,1)S(1)}, bf16[256,2048]{1,0:T(8,128)(2,1)}, u32[]{:S(2)}) copy-start(bf16[256,2048]{1,0:T(8,128)(2,1)} %param.3) | copy-start | bytes 3145732
  7.2 52.2 %all-gather.5.cloned.1.call-start = ((), (), s32[]{:S(2)}) async-start(), calls=%async_computation.3 | async-start | bytes 2621440 | tf_op jit(solution)/shard_map/all_gather | solution.py:167
  10.6 72.3 %all-gather.3.cloned.1.call-start = ((), (), s32[]{:S(2)}) async-start(), calls=%async_computation.2 | async-start | bytes 2621440 | tf_op jit(solution)/shard_map/all_gather | solution.py:166
  11.3 108.4 %reduce-scatter.3.cloned.1.call-start = ((), (), s32[]{:S(2)}) async-start(), calls=%async_computation.4 | async-start | bytes 2621440 | tf_op jit(solution)/shard_map/reduce_scatter | solution.py:199
  88.1 77.8 %reduce-scatter.5.cloned.1.call-start = ((), (), s32[]{:S(2)}) async-start(), calls=%async_computation.5 | async-start | bytes 2621440 | tf_op jit(solution)/shard_map/reduce_scatter | solution.py:199
  90.4 2.6 %copy-start.2 = (bf16[512,2048]{1,0:T(8,128)(2,1)S(1)}, bf16[512,2048]{1,0:T(8,128)(2,1)}, u32[]{:S(2)}) copy-start(bf16[512,2048]{1,0:T(8,128)(2,1)} %all-gather.5.cloned.1.call-done) | copy-start | bytes 6291460
  94.0 71.9 %copy-start.1 = (bf16[128,2048]{1,0:T(8,128)(2,1)S(1)}, bf16[128,2048]{1,0:T(8,128)(2,1)}, u32[]{:S(2)}) copy-start(bf16[128,2048]{1,0:T(8,128)(2,1)} %param.4) | copy-start | bytes 1572868
Sparse Core Ops, SparseCore 0:
  10.7 48.6 all-gather.4
  61.5 21.2 all-gather.2
  88.3 31.4 reduce-scatter.2
  122.0 43.8 reduce-scatter.4

commit v2 on v1

--- a/solution.py
+++ b/solution.py
@@ -1,6 +1,10 @@
+import functools
+
 import jax
 import jax.numpy as jnp
 from jax import lax
+from jax.experimental import pallas as pl
+from jax.experimental.pallas import tpu as pltpu
 from jax.sharding import PartitionSpec as P
 
 sharpness_factor = 20.0
@@ -208,8 +212,322 @@
     )
 
 
+CHUNKS = 2
+ROWS = 32
+MESH = pl.DeviceIdType.MESH
+
+
+def dot(left, right, left_dim, right_dim):
+    return lax.dot_general(
+        left,
+        right,
+        (((left_dim,), (right_dim,)), ((), ())),
+        preferred_element_type=jnp.float32,
+    )
+
+
+def fused_kernel(
+    nb, ng,
+    queries, passages, owners,
+    loss_out, query_out, passage_out,
+    line, group, query_half, query_norm, passage_norm,
+    grad_in, grad_hard, query_dir,
+    hard_sums, from_left, from_right, in_sums, from_group,
+    gather_send, gather_recv, group_send, group_recv,
+    reduce_send, reduce_recv, back_send, back_recv,
+):
+    b = lax.axis_index("batch")
+    g = lax.axis_index("grp")
+    rows, width = queries.shape
+    block = passages.shape[0]
+    part = block // CHUNKS
+    last = nb - 1
+
+    def when(condition, act):
+        pl.when(condition)(act)
+
+    def piece(c):
+        return pl.ds(c * part, part)
+
+    def along(src, dst, send, recv, step):
+        return pltpu.make_async_remote_copy(
+            src_ref=src, dst_ref=dst, send_sem=send, recv_sem=recv,
+            device_id={"batch": b + step}, device_id_type=MESH,
+        )
+
+    def gather(way, owner, s, c):
+        ref = line.at[owner, piece(c)]
+        return along(ref, ref, gather_send.at[way, s, c], gather_recv.at[way, s, c], 1 - 2 * way)
+
+    def group_copy(src, dst, send, recv, k):
+        return pltpu.make_async_remote_copy(
+            src_ref=src, dst_ref=dst, send_sem=send.at[k], recv_sem=recv.at[k],
+            device_id={"grp": lax.rem(g + k, ng)}, device_id_type=MESH,
+        )
+
+    def reduce(way, s, c):
+        target = s if way else last - s
+        landing = from_right if way else from_left
+        return along(
+            hard_sums.at[target, piece(c)], landing.at[s, piece(c)],
+            reduce_send.at[way, s, c], reduce_recv.at[way, s, c], 1 - 2 * way,
+        )
+
+    barrier = pltpu.get_barrier_semaphore()
+
+    def greet(step):
+        pl.semaphore_signal(
+            barrier, inc=1, device_id={"batch": b + step}, device_id_type=MESH
+        )
+
+    when(b > 0, lambda: greet(-1))
+    when(b < last, lambda: greet(1))
+    for k in range(1, ng):
+        pl.semaphore_signal(
+            barrier, inc=1, device_id={"grp": lax.rem(g + k, ng)}, device_id_type=MESH
+        )
+
+    def norm_passages(i, _):
+        at = pl.ds(pl.multiple_of(i * ROWS, ROWS), ROWS)
+        wide = passages[at, :].astype(jnp.float32)
+        norm = lax.rsqrt(jnp.sum(wide * wide, axis=1, keepdims=True) + norm_eps)
+        half = (wide * norm).astype(jnp.bfloat16)
+        passage_norm[at, :] = norm
+        line[b, at, :] = half
+        group[g, at, :] = half
+        return _
+
+    lax.fori_loop(0, block // ROWS, norm_passages, 0)
+    pl.semaphore_wait(
+        barrier, ng - 1 + (b > 0).astype(jnp.int32) + (b < last).astype(jnp.int32)
+    )
+    for c in range(CHUNKS):
+        when(b < last, lambda: gather(0, b, 0, c).start())
+        when(b > 0, lambda: gather(1, b, 0, c).start())
+    for k in range(1, ng):
+        group_copy(group.at[g], group.at[g], group_send, group_recv, k).start()
+
+    def norm_queries(i, _):
+        at = pl.ds(pl.multiple_of(i * ROWS, ROWS), ROWS)
+        wide = queries[at, :].astype(jnp.float32)
+        norm = lax.rsqrt(jnp.sum(wide * wide, axis=1, keepdims=True) + norm_eps)
+        query_norm[at, :] = norm
+        query_half[at, :] = (wide * norm).astype(jnp.bfloat16)
+        return _
+
+    lax.fori_loop(0, rows // ROWS, norm_queries, 0)
+
+    def take(way, s, c):
+        owner = b + 1 + s if way else b - 1 - s
+
+        def pass_on():
+            gather(way, owner, s + 1, c).start()
+
+        def arrive():
+            gather(way, owner, s, c).wait_recv()
+            if s + 1 < last:
+                when(b > 0 if way else b < last, pass_on)
+
+        when(owner <= last if way else owner >= 0, arrive)
+
+    for s in range(last):
+        for c in range(CHUNKS):
+            take(0, s, c)
+            take(1, s, c)
+    for k in range(1, ng):
+        source = lax.rem(g + ng - k, ng)
+        group_copy(
+            group.at[source], group.at[source], group_send, group_recv, k
+        ).wait_recv()
+
+    units = query_half[...]
+    scores_in = sharpness_factor * dot(
+        units, group[...].reshape(ng * block, width), 1, 1
+    )
+    scores_hard = sharpness_factor * dot(
+        units, line[...].reshape(nb * block, width), 1, 1
+    )
+    raised_in = jnp.exp(scores_in)
+    names = owners[...]
+    raised_hard = []
+    for n in range(nb):
+        named = jnp.any(names == n, axis=1, keepdims=True)
+        raised_hard.append(
+            jnp.where(named, jnp.exp(scores_hard[:, n * block:(n + 1) * block]), 0.0)
+        )
+    totals = jnp.sum(raised_in, axis=1, keepdims=True) + jnp.sum(
+        functools.reduce(jnp.add, raised_hard), axis=1, keepdims=True
+    )
+    shape = (rows, ng * block)
+    column = g * block + lax.rem(lax.broadcasted_iota(jnp.int32, shape, 0), block)
+    positive = lax.broadcasted_iota(jnp.int32, shape, 1) == column
+    losses = jnp.log(totals) - jnp.sum(
+        jnp.where(positive, scores_in, 0.0), axis=1, keepdims=True
+    )
+    square = (block, block)
+    diagonal = lax.broadcasted_iota(jnp.int32, square, 0) == lax.broadcasted_iota(
+        jnp.int32, square, 1
+    )
+    for i in range(rows // block):
+        loss_out[i:i + 1, :] = jnp.sum(
+            jnp.where(diagonal, losses[i * block:(i + 1) * block], 0.0), axis=0, keepdims=True
+        )
+    scale = sharpness_factor / totals
+    for n in range(nb):
+        grad_hard[:, n * block:(n + 1) * block] = (raised_hard[n] * scale).astype(jnp.bfloat16)
+    grad_in[...] = (
+        raised_in * scale - jnp.where(positive, sharpness_factor, 0.0)
+    ).astype(jnp.bfloat16)
+
+    for n in sorted(range(nb), key=lambda n: -abs(2 * n - last)):
+        hard_sums[n] = dot(
+            grad_hard[:, n * block:(n + 1) * block], query_half[...], 0, 0
+        ).astype(jnp.bfloat16)
+        for c in range(CHUNKS):
+            if n > 0:
+                when(b == 0, lambda: reduce(0, last - n, c).start())
+            if n < last:
+                when(b == last, lambda: reduce(1, n, c).start())
+    for h in range(ng):
+        in_sums[h] = dot(
+            grad_in[:, h * block:(h + 1) * block], query_half[...], 0, 0
+        ).astype(jnp.bfloat16)
+
+    def back_copy(k):
+        return group_copy(
+            in_sums.at[lax.rem(g + k, ng)], from_group.at[k - 1], back_send, back_recv, k
+        )
+
+    for k in range(1, ng):
+        back_copy(k).start()
+
+    tile = min(512, width)
+    for j in range(0, width, tile):
+        query_dir[:, j:j + tile] = dot(
+            grad_in[...], group[:, :, j:j + tile].reshape(ng * block, tile), 1, 0
+        ) + dot(grad_hard[...], line[:, :, j:j + tile].reshape(nb * block, tile), 1, 0)
+
+    def finish_queries(i, _):
+        at = pl.ds(pl.multiple_of(i * ROWS, ROWS), ROWS)
+        norm = query_norm[at, :]
+        unit = queries[at, :].astype(jnp.float32) * norm
+        direction = query_dir[at, :]
+        inner = jnp.sum(unit * direction, axis=1, keepdims=True)
+        query_out[at, :] = (norm * (direction - unit * inner)).astype(jnp.bfloat16)
+        return _
+
+    lax.fori_loop(0, rows // ROWS, finish_queries, 0)
+
+    def add_and_pass(way, s, c):
+        target = s if way else last - s
+        landing = from_right if way else from_left
+
+        def act():
+            reduce(way, s, c).wait_recv()
+            own = hard_sums[target, piece(c), :].astype(jnp.float32)
+            hard_sums[target, piece(c), :] = (
+                own + landing[s, piece(c), :].astype(jnp.float32)
+            ).astype(jnp.bfloat16)
+            reduce(way, s, c).start()
+
+        when((b < last) & (b > target) if way else (b > 0) & (b < target), act)
+
+    for s in range(last):
+        for c in range(CHUNKS):
+            add_and_pass(0, s, c)
+            add_and_pass(1, s, c)
+    for k in range(1, ng):
+        back_copy(k).wait_recv()
+
+    def finish_passages(at):
+        total = hard_sums[b, at, :].astype(jnp.float32) + in_sums[g, at, :].astype(jnp.float32)
+        for k in range(ng - 1):
+            total += from_group[k, at, :].astype(jnp.float32)
+        return total
+
+    left_at = jnp.minimum(last - b, last - 1)
+    right_at = jnp.minimum(b, last - 1)
+    for c in range(CHUNKS):
+        for way in (0, 1):
+            for s in range(last):
+                target = s if way else last - s
+                when(b == target, lambda: reduce(way, s, c).wait_recv())
+
+        def finish(i, _):
+            at = pl.ds(pl.multiple_of(c * part + i * ROWS, ROWS), ROWS)
+            direction = finish_passages(at)
+            direction += jnp.where(b > 0, from_left[left_at, at, :].astype(jnp.float32), 0.0)
+            direction += jnp.where(b < last, from_right[right_at, at, :].astype(jnp.float32), 0.0)
+            norm = passage_norm[at, :]
+            unit = passages[at, :].astype(jnp.float32) * norm
+            inner = jnp.sum(unit * direction, axis=1, keepdims=True)
+            passage_out[at, :] = (norm * (direction - unit * inner)).astype(jnp.bfloat16)
+            return _
+
+        lax.fori_loop(0, part // ROWS, finish, 0)
+
+    for s in range(last):
+        for c in range(CHUNKS):
+            when((b < last) & (b >= s), lambda: gather(0, b - s, s, c).wait_send())
+            when((b > 0) & (b + s <= last), lambda: gather(1, b + s, s, c).wait_send())
+            when(b < last - s, lambda: reduce(0, s, c).wait_send())
+            when(b > s, lambda: reduce(1, s, c).wait_send())
+    for k in range(1, ng):
+        group_copy(group.at[g], group.at[g], group_send, group_recv, k).wait_send()
+        back_copy(k).wait_send()
+
+
+def local_fused(queries, passages, hard_owners):
+    rows, width = queries.shape
+    block = passages.shape[0]
+    nb, ng = lax.axis_size("batch"), lax.axis_size("grp")
+    half, wide = jnp.bfloat16, jnp.float32
+    vmem = pl.BlockSpec(memory_space=pltpu.VMEM)
+    line_sems = pltpu.SemaphoreType.DMA((2, nb - 1, CHUNKS))
+    group_sems = pltpu.SemaphoreType.DMA((ng,))
+    loss, query_grad, passage_grad = pl.pallas_call(
+        functools.partial(fused_kernel, nb, ng),
+        out_shape=(
+            jax.ShapeDtypeStruct((rows // block, block), wide),
+            jax.ShapeDtypeStruct((rows, width), half),
+            jax.ShapeDtypeStruct((block, width), half),
+        ),
+        in_specs=[vmem] * 3,
+        out_specs=(vmem,) * 3,
+        scratch_shapes=[
+            pltpu.VMEM((nb, block, width), half),
+            pltpu.VMEM((ng, block, width), half),
+            pltpu.VMEM((rows, width), half),
+            pltpu.VMEM((rows, 1), wide),
+            pltpu.VMEM((block, 1), wide),
+            pltpu.VMEM((rows, ng * block), half),
+            pltpu.VMEM((rows, nb * block), half),
+            pltpu.VMEM((rows, width), wide),
+            pltpu.VMEM((nb, block, width), half),
+            pltpu.VMEM((nb - 1, block, width), half),
+            pltpu.VMEM((nb - 1, block, width), half),
+            pltpu.VMEM((ng, block, width), half),
+            pltpu.VMEM((ng - 1, block, width), half),
+            line_sems, line_sems, group_sems, group_sems,
+            line_sems, line_sems, group_sems, group_sems,
+        ],
+        compiler_params=pltpu.CompilerParams(
+            collective_id=0, has_side_effects=True, vmem_limit_bytes=48 * 1024 * 1024
+        ),
+        cost_estimate=pl.CostEstimate(
+            flops=6 * rows * (nb + ng) * block * width,
+            bytes_accessed=4 * (rows + block) * width,
+            transcendentals=rows * (nb + ng) * block,
+        ),
+    )(queries, passages, hard_owners)
+    return (loss.reshape(-1), query_grad, passage_grad)
+
+
 def local(queries, passages, hard_owners):
-    if lax.axis_size("batch") <= 8:
+    nb = lax.axis_size("batch")
+    if 1 < nb <= 8 and 1 < lax.axis_size("grp") <= 8:
+        return local_fused(queries, passages, hard_owners)
+    if nb <= 8:
         return local_dense(queries, passages, hard_owners)
     return local_slots(queries, passages, hard_owners)
 

time: 177 us -> 90.3 us (0.51)
  the two profiles are of different devices: /device:TPU:0 before, /device:TPU:20 now
where the time goes in v2:
time: 90.3 us; the launch traced here: 90 us
  Pallas kernels  84 us (93%)
  local copies, waits for them, and re-layouts  5.4 us (6%)
    pallas_call x1, Pallas kernels, local_fused(): pl.pallas_call(functools.partial(fused_kernel, nb, ng), out_shape=(jax.Sh...  84 us
    unnamed x8, local copies, waits for them, and re-layouts  5.4 us

profile of v2, /device:TPU:20, one launch (start us, length us, event | category | flops | bytes accessed | tf_op | source)
XLA Modules:
  0.0 90.0 jit_solution(8981488850040535115)
XLA Ops:
  0.6 0.8 copy.6.owners
  1.4 0.0 copy-start
  1.5 1.2 %copy-done = bf16[256,2048]{1,0:T(8,128)(2,1)S(1)} copy-done((bf16[256,2048]{1,0:T(8,128)(2,1)S(1)}, bf16[256,2048]{1,0:T(8,128)(2,1)}, u32[]{:S(2)}) %copy-start) | copy-done | bytes 1048600
  2.7 0.0 copy-start.1
  2.7 1.0 %copy-done.1 = bf16[128,2048]{1,0:T(8,128)(2,1)S(1)} copy-done((bf16[128,2048]{1,0:T(8,128)(2,1)S(1)}, bf16[128,2048]{1,0:T(8,128)(2,1)}, u32[]{:S(2)}) %copy-start.1) | copy-done | bytes 524312
  3.7 84.0 %shard_map.58 = (f32[2,128]{1,0:T(2,128)S(1)}, bf16[256,2048]{1,0:T(8,128)(2,1)S(1)}, bf16[128,2048]{1,0:T(8,128)(2,1)S(1)}) custom-call(bf16[256,2048]{1,0:T(8,128)(2,1)S(1)} %copy-done, bf16[128,2048]{1,0:T(8,128)(2,1)S(1)} %copy-done.1, s32[256,2]{1,0:T(8,128)S(1)} %copy.6.owners), custom_call_target="tpu_custom_call" | custom-call | flops 3221225472 | bytes 3145728 | tf_op jit(solution)/shard_map/pallas_call | solution.py:488
  87.7 0.6 copy.10
  88.3 1.0 %copy.11 = bf16[256,2048]{1,0:T(8,128)(2,1)} copy(bf16[256,2048]{1,0:T(8,128)(2,1)S(1)} %get-tuple-element.13) | data formatting | bytes 2097152
  89.3 0.8 copy.12
Async XLA Ops:
  1.4 1.2 %copy-start = (bf16[256,2048]{1,0:T(8,128)(2,1)S(1)}, bf16[256,2048]{1,0:T(8,128)(2,1)}, u32[]{:S(2)}) copy-start(bf16[256,2048]{1,0:T(8,128)(2,1)} %queries.1) | copy-start | bytes 3145732
  2.7 1.0 %copy-start.1 = (bf16[128,2048]{1,0:T(8,128)(2,1)S(1)}, bf16[128,2048]{1,0:T(8,128)(2,1)}, u32[]{:S(2)}) copy-start(bf16[128,2048]{1,0:T(8,128)(2,1)} %passages.1) | copy-start | bytes 1572868

commit v3 on v2

--- a/solution.py
+++ b/solution.py
@@ -228,11 +228,13 @@
 
 def fused_kernel(
     nb, ng,
-    queries, passages, owners,
+    queries_far, passages_far, owners,
     loss_out, query_out, passage_out,
-    line, group, query_half, query_norm, passage_norm,
+    queries, passages, line, group, query_half, query_norm, passage_norm,
     grad_in, grad_hard, query_dir,
     hard_sums, from_left, from_right, in_sums, from_group,
+    hard_parts, guest, guest_hard,
+    load_sems, guest_send, guest_recv, weight_send, weight_recv,
     gather_send, gather_recv, group_send, group_recv,
     reduce_send, reduce_recv, back_send, back_recv,
 ):
@@ -273,6 +275,26 @@
             reduce_send.at[way, s, c], reduce_recv.at[way, s, c], 1 - 2 * way,
         )
 
+    inward = jnp.where(b == 0, 1, -1)
+
+    def guest_copy(c):
+        half = pl.ds(c * (rows // 2), rows // 2)
+        return along(
+            query_half.at[half], guest.at[half], guest_send.at[c], guest_recv.at[c], inward
+        )
+
+    def weight_copy(s):
+        target = jnp.where(b == 0, last - s, s)
+        return along(
+            hard_parts.at[target], guest_hard.at[s], weight_send.at[s], weight_recv.at[s], inward
+        )
+
+    load_passages = pltpu.make_async_copy(passages_far, passages, load_sems.at[0])
+    load_queries = pltpu.make_async_copy(queries_far, queries, load_sems.at[1])
+    load_passages.start()
+    load_queries.start()
+    end = (b == 0) | (b == last)
+    host = (b == 1) | (b == last - 1)
     barrier = pltpu.get_barrier_semaphore()
 
     def greet(step):
@@ -297,6 +319,7 @@
         group[g, at, :] = half
         return _
 
+    load_passages.wait()
     lax.fori_loop(0, block // ROWS, norm_passages, 0)
     pl.semaphore_wait(
         barrier, ng - 1 + (b > 0).astype(jnp.int32) + (b < last).astype(jnp.int32)
@@ -315,7 +338,10 @@
         query_half[at, :] = (wide * norm).astype(jnp.bfloat16)
         return _
 
+    load_queries.wait()
     lax.fori_loop(0, rows // ROWS, norm_queries, 0)
+    for c in range(2):
+        when(end, lambda: guest_copy(c).start())
 
     def take(way, s, c):
         owner = b + 1 + s if way else b - 1 - s
@@ -348,33 +374,51 @@
         units, line[...].reshape(nb * block, width), 1, 1
     )
     raised_in = jnp.exp(scores_in)
-    names = owners[...]
+    square = (block, block)
+    diagonal = lax.broadcasted_iota(jnp.int32, square, 0) == lax.broadcasted_iota(
+        jnp.int32, square, 1
+    )
+
+    def upright(row):
+        pieces = [
+            jnp.sum(
+                jnp.where(diagonal, row[:, i * block:(i + 1) * block], 0.0),
+                axis=1,
+                keepdims=True,
+            )
+            for i in range(rows // block)
+        ]
+        return jnp.concatenate(pieces, axis=0)
+
+    names = [
+        upright(owners[k:k + 1, :].astype(jnp.float32)) for k in range(owners.shape[0])
+    ]
     raised_hard = []
     for n in range(nb):
-        named = jnp.any(names == n, axis=1, keepdims=True)
+        named = functools.reduce(jnp.logical_or, [name == n for name in names])
         raised_hard.append(
             jnp.where(named, jnp.exp(scores_hard[:, n * block:(n + 1) * block]), 0.0)
         )
     totals = jnp.sum(raised_in, axis=1, keepdims=True) + jnp.sum(
         functools.reduce(jnp.add, raised_hard), axis=1, keepdims=True
     )
+    scale = sharpness_factor / totals
+    for n in range(nb):
+        weights = (raised_hard[n] * scale).astype(jnp.bfloat16)
+        grad_hard[:, n * block:(n + 1) * block] = weights
+        hard_parts[n] = weights
+    for s in range(last):
+        when(end, lambda: weight_copy(s).start())
     shape = (rows, ng * block)
     column = g * block + lax.rem(lax.broadcasted_iota(jnp.int32, shape, 0), block)
     positive = lax.broadcasted_iota(jnp.int32, shape, 1) == column
     losses = jnp.log(totals) - jnp.sum(
         jnp.where(positive, scores_in, 0.0), axis=1, keepdims=True
     )
-    square = (block, block)
-    diagonal = lax.broadcasted_iota(jnp.int32, square, 0) == lax.broadcasted_iota(
-        jnp.int32, square, 1
-    )
     for i in range(rows // block):
         loss_out[i:i + 1, :] = jnp.sum(
             jnp.where(diagonal, losses[i * block:(i + 1) * block], 0.0), axis=0, keepdims=True
         )
-    scale = sharpness_factor / totals
-    for n in range(nb):
-        grad_hard[:, n * block:(n + 1) * block] = (raised_hard[n] * scale).astype(jnp.bfloat16)
     grad_in[...] = (
         raised_in * scale - jnp.where(positive, sharpness_factor, 0.0)
     ).astype(jnp.bfloat16)
@@ -383,11 +427,6 @@
         hard_sums[n] = dot(
             grad_hard[:, n * block:(n + 1) * block], query_half[...], 0, 0
         ).astype(jnp.bfloat16)
-        for c in range(CHUNKS):
-            if n > 0:
-                when(b == 0, lambda: reduce(0, last - n, c).start())
-            if n < last:
-                when(b == last, lambda: reduce(1, n, c).start())
     for h in range(ng):
         in_sums[h] = dot(
             grad_in[:, h * block:(h + 1) * block], query_half[...], 0, 0
@@ -430,9 +469,30 @@
             ).astype(jnp.bfloat16)
             reduce(way, s, c).start()
 
-        when((b < last) & (b > target) if way else (b > 0) & (b < target), act)
-
-    for s in range(last):
+        when((b < last - 1) & (b > target) if way else (b > 1) & (b < target), act)
+
+    def add_guest(s):
+        target = jnp.where(b == 1, last - s, s)
+        weight_copy(s).wait_recv()
+        for j in range(0, width, tile):
+            cols = pl.ds(j, tile)
+            own = hard_sums[target, :, cols].astype(jnp.float32)
+            hard_sums[target, :, cols] = (
+                own + dot(guest_hard[s], guest[:, cols], 0, 0)
+            ).astype(jnp.bfloat16)
+        if s < last - 1:
+            for c in range(CHUNKS):
+                when(b == 1, lambda: reduce(0, s, c).start())
+                when(b == last - 1, lambda: reduce(1, s, c).start())
+
+    def serve():
+        for c in range(2):
+            guest_copy(c).wait_recv()
+        for s in range(last):
+            add_guest(s)
+
+    when(host, serve)
+    for s in range(last - 1):
         for c in range(CHUNKS):
             add_and_pass(0, s, c)
             add_and_pass(1, s, c)
@@ -445,19 +505,19 @@
             total += from_group[k, at, :].astype(jnp.float32)
         return total
 
-    left_at = jnp.minimum(last - b, last - 1)
-    right_at = jnp.minimum(b, last - 1)
+    left_at = jnp.minimum(last - b, last - 2)
+    right_at = jnp.minimum(b, last - 2)
     for c in range(CHUNKS):
         for way in (0, 1):
-            for s in range(last):
+            for s in range(last - 1):
                 target = s if way else last - s
                 when(b == target, lambda: reduce(way, s, c).wait_recv())
 
         def finish(i, _):
             at = pl.ds(pl.multiple_of(c * part + i * ROWS, ROWS), ROWS)
             direction = finish_passages(at)
-            direction += jnp.where(b > 0, from_left[left_at, at, :].astype(jnp.float32), 0.0)
-            direction += jnp.where(b < last, from_right[right_at, at, :].astype(jnp.float32), 0.0)
+            direction += jnp.where(b > 1, from_left[left_at, at, :].astype(jnp.float32), 0.0)
+            direction += jnp.where(b < last - 1, from_right[right_at, at, :].astype(jnp.float32), 0.0)
             norm = passage_norm[at, :]
             unit = passages[at, :].astype(jnp.float32) * norm
             inner = jnp.sum(unit * direction, axis=1, keepdims=True)
@@ -470,8 +530,12 @@
         for c in range(CHUNKS):
             when((b < last) & (b >= s), lambda: gather(0, b - s, s, c).wait_send())
             when((b > 0) & (b + s <= last), lambda: gather(1, b + s, s, c).wait_send())
-            when(b < last - s, lambda: reduce(0, s, c).wait_send())
-            when(b > s, lambda: reduce(1, s, c).wait_send())
+            if s < last - 1:
+                when((b > 0) & (b < last - s), lambda: reduce(0, s, c).wait_send())
+                when((b < last) & (b > s), lambda: reduce(1, s, c).wait_send())
+        when(end, lambda: weight_copy(s).wait_send())
+    for c in range(2):
+        when(end, lambda: guest_copy(c).wait_send())
     for k in range(1, ng):
         group_copy(group.at[g], group.at[g], group_send, group_recv, k).wait_send()
         back_copy(k).wait_send()
@@ -483,7 +547,11 @@
     nb, ng = lax.axis_size("batch"), lax.axis_size("grp")
     half, wide = jnp.bfloat16, jnp.float32
     vmem = pl.BlockSpec(memory_space=pltpu.VMEM)
+    far = pl.BlockSpec(memory_space=pl.ANY)
     line_sems = pltpu.SemaphoreType.DMA((2, nb - 1, CHUNKS))
+    sum_sems = pltpu.SemaphoreType.DMA((2, nb - 2, CHUNKS))
+    pair_sems = pltpu.SemaphoreType.DMA((2,))
+    weight_sems = pltpu.SemaphoreType.DMA((nb - 1,))
     group_sems = pltpu.SemaphoreType.DMA((ng,))
     loss, query_grad, passage_grad = pl.pallas_call(
         functools.partial(fused_kernel, nb, ng),
@@ -492,9 +560,11 @@
             jax.ShapeDtypeStruct((rows, width), half),
             jax.ShapeDtypeStruct((block, width), half),
         ),
-        in_specs=[vmem] * 3,
+        in_specs=[far, far, vmem],
         out_specs=(vmem,) * 3,
         scratch_shapes=[
+            pltpu.VMEM((rows, width), half),
+            pltpu.VMEM((block, width), half),
             pltpu.VMEM((nb, block, width), half),
             pltpu.VMEM((ng, block, width), half),
             pltpu.VMEM((rows, width), half),
@@ -504,28 +574,32 @@
             pltpu.VMEM((rows, nb * block), half),
             pltpu.VMEM((rows, width), wide),
             pltpu.VMEM((nb, block, width), half),
-            pltpu.VMEM((nb - 1, block, width), half),
-            pltpu.VMEM((nb - 1, block, width), half),
+            pltpu.VMEM((nb - 2, block, width), half),
+            pltpu.VMEM((nb - 2, block, width), half),
             pltpu.VMEM((ng, block, width), half),
             pltpu.VMEM((ng - 1, block, width), half),
+            pltpu.VMEM((nb, rows, block), half),
+            pltpu.VMEM((rows, width), half),
+            pltpu.VMEM((nb - 1, rows, block), half),
+            pair_sems, pair_sems, pair_sems, weight_sems, weight_sems,
             line_sems, line_sems, group_sems, group_sems,
-            line_sems, line_sems, group_sems, group_sems,
+            sum_sems, sum_sems, group_sems, group_sems,
         ],
         compiler_params=pltpu.CompilerParams(
-            collective_id=0, has_side_effects=True, vmem_limit_bytes=48 * 1024 * 1024
+            collective_id=0, has_side_effects=True, vmem_limit_bytes=56 * 1024 * 1024
         ),
         cost_estimate=pl.CostEstimate(
             flops=6 * rows * (nb + ng) * block * width,
             bytes_accessed=4 * (rows + block) * width,
             transcendentals=rows * (nb + ng) * block,
         ),
-    )(queries, passages, hard_owners)
+    )(queries, passages, hard_owners.T)
     return (loss.reshape(-1), query_grad, passage_grad)
 
 
 def local(queries, passages, hard_owners):
     nb = lax.axis_size("batch")
-    if 1 < nb <= 8 and 1 < lax.axis_size("grp") <= 8:
+    if 4 <= nb <= 8 and 1 < lax.axis_size("grp") <= 8:
         return local_fused(queries, passages, hard_owners)
     if nb <= 8:
         return local_dense(queries, passages, hard_owners)

time: 90.3 us -> 74.5 us (0.83)
  the two profiles are of different devices: /device:TPU:20 before, /device:TPU:8 now
where the time goes in v3:
time: 74.5 us; the launch traced here: 74.3 us
  Pallas kernels  69.2 us (93%)
  local copies, waits for them, and re-layouts  4.38 us (6%)
    pallas_call x1, Pallas kernels, local_fused(): pl.pallas_call(functools.partial(fused_kernel, nb, ng), out_shape=(jax.Sh...  69.2 us
    unnamed x7, local copies, waits for them, and re-layouts  4.38 us

profile of v3, /device:TPU:8, one launch (start us, length us, event | category | flops | bytes accessed | tf_op | source)
XLA Modules:
  0.0 74.3 jit_solution(17616604553279967204)
XLA Ops:
  0.6 69.2 %shard_map.58 = (f32[2,128]{1,0:T(2,128)}, bf16[256,2048]{1,0:T(8,128)(2,1)}, bf16[128,2048]{1,0:T(8,128)(2,1)}) custom-call(bf16[256,2048]{1,0:T(8,128)(2,1)} %queries_far.1, bf16[128,2048]{1,0:T(8,128)(2,1)} %passages_far.1, s32[2,256]{1,0:T(2,128)} %bitcast.3), custom_call_target="tpu_custom_call" | custom-call | flops 3221225472 | bytes 3145728 | tf_op jit(solution)/shard_map/pallas_call | solution.py:556
  69.9 0.0 copy-start.1
  69.9 0.7 copy-done.1
  70.5 0.6 copy.9
  71.1 0.0 copy-start
  71.1 2.4 %copy.10 = bf16[256,2048]{1,0:T(8,128)(2,1)} copy(bf16[256,2048]{1,0:T(8,128)(2,1)} %get-tuple-element.13) | data formatting | bytes 2097152
  73.5 0.0 copy-done
  73.5 0.8 %copy.11 = bf16[128,2048]{1,0:T(8,128)(2,1)} copy(bf16[128,2048]{1,0:T(8,128)(2,1)S(1)} %copy-done) | data formatting | bytes 1048576
Async XLA Ops:
  69.9 0.7 copy-start.1
  71.1 2.4 %copy-start = (bf16[128,2048]{1,0:T(8,128)(2,1)S(1)}, bf16[128,2048]{1,0:T(8,128)(2,1)}, u32[]{:S(2)}) copy-start(bf16[128,2048]{1,0:T(8,128)(2,1)} %get-tuple-element.14) | copy-start | bytes 1572868

commit v4 on v3

--- a/solution.py
+++ b/solution.py
@@ -212,7 +212,8 @@
     )
 
 
-CHUNKS = 2
+GATHER_CHUNKS = 2
+SUM_CHUNKS = 2
 ROWS = 32
 MESH = pl.DeviceIdType.MESH
 
@@ -234,6 +235,7 @@
     grad_in, grad_hard, query_dir,
     hard_sums, from_left, from_right, in_sums, from_group,
     hard_parts, guest, guest_hard,
+    names, raised_hard, hard_total, raised_in, in_total, positive_score,
     load_sems, guest_send, guest_recv, weight_send, weight_recv,
     gather_send, gather_recv, group_send, group_recv,
     reduce_send, reduce_recv, back_send, back_recv,
@@ -242,14 +244,14 @@
     g = lax.axis_index("grp")
     rows, width = queries.shape
     block = passages.shape[0]
-    part = block // CHUNKS
+    tile = min(512, width)
     last = nb - 1
 
     def when(condition, act):
         pl.when(condition)(act)
 
-    def piece(c):
-        return pl.ds(c * part, part)
+    def piece(c, count):
+        return pl.ds(c * (block // count), block // count)
 
     def along(src, dst, send, recv, step):
         return pltpu.make_async_remote_copy(
@@ -258,7 +260,7 @@
         )
 
     def gather(way, owner, s, c):
-        ref = line.at[owner, piece(c)]
+        ref = line.at[owner, piece(c, GATHER_CHUNKS)]
         return along(ref, ref, gather_send.at[way, s, c], gather_recv.at[way, s, c], 1 - 2 * way)
 
     def group_copy(src, dst, send, recv, k):
@@ -271,7 +273,7 @@
         target = s if way else last - s
         landing = from_right if way else from_left
         return along(
-            hard_sums.at[target, piece(c)], landing.at[s, piece(c)],
+            hard_sums.at[target, piece(c, SUM_CHUNKS)], landing.at[s, piece(c, SUM_CHUNKS)],
             reduce_send.at[way, s, c], reduce_recv.at[way, s, c], 1 - 2 * way,
         )
 
@@ -324,7 +326,7 @@
     pl.semaphore_wait(
         barrier, ng - 1 + (b > 0).astype(jnp.int32) + (b < last).astype(jnp.int32)
     )
-    for c in range(CHUNKS):
+    for c in range(GATHER_CHUNKS):
         when(b < last, lambda: gather(0, b, 0, c).start())
         when(b > 0, lambda: gather(1, b, 0, c).start())
     for k in range(1, ng):
@@ -356,24 +358,6 @@
 
         when(owner <= last if way else owner >= 0, arrive)
 
-    for s in range(last):
-        for c in range(CHUNKS):
-            take(0, s, c)
-            take(1, s, c)
-    for k in range(1, ng):
-        source = lax.rem(g + ng - k, ng)
-        group_copy(
-            group.at[source], group.at[source], group_send, group_recv, k
-        ).wait_recv()
-
-    units = query_half[...]
-    scores_in = sharpness_factor * dot(
-        units, group[...].reshape(ng * block, width), 1, 1
-    )
-    scores_hard = sharpness_factor * dot(
-        units, line[...].reshape(nb * block, width), 1, 1
-    )
-    raised_in = jnp.exp(scores_in)
     square = (block, block)
     diagonal = lax.broadcasted_iota(jnp.int32, square, 0) == lax.broadcasted_iota(
         jnp.int32, square, 1
@@ -390,18 +374,47 @@
         ]
         return jnp.concatenate(pieces, axis=0)
 
-    names = [
-        upright(owners[k:k + 1, :].astype(jnp.float32)) for k in range(owners.shape[0])
-    ]
-    raised_hard = []
-    for n in range(nb):
-        named = functools.reduce(jnp.logical_or, [name == n for name in names])
-        raised_hard.append(
-            jnp.where(named, jnp.exp(scores_hard[:, n * block:(n + 1) * block]), 0.0)
-        )
-    totals = jnp.sum(raised_in, axis=1, keepdims=True) + jnp.sum(
-        functools.reduce(jnp.add, raised_hard), axis=1, keepdims=True
-    )
+    for k in range(owners.shape[0]):
+        names[k] = upright(owners[k:k + 1, :].astype(jnp.float32))
+
+    def score(n):
+        raised = jnp.exp(sharpness_factor * dot(query_half[...], line[n], 1, 1))
+        named = functools.reduce(
+            jnp.logical_or,
+            [names[k] == n.astype(jnp.float32) for k in range(owners.shape[0])],
+        )
+        raised = jnp.where(named, raised, 0.0)
+        raised_hard[n] = raised
+        hard_total[...] += raised
+
+    hard_total[...] = jnp.zeros_like(hard_total)
+    score(b)
+    shape = (rows, ng * block)
+    column = g * block + lax.rem(lax.broadcasted_iota(jnp.int32, shape, 0), block)
+    for s in range(last):
+        if s == last - 1:
+            for k in range(1, ng):
+                source = lax.rem(g + ng - k, ng)
+                group_copy(
+                    group.at[source], group.at[source], group_send, group_recv, k
+                ).wait_recv()
+            scores_in = sharpness_factor * dot(
+                query_half[...], group[...].reshape(ng * block, width), 1, 1
+            )
+            raised = jnp.exp(scores_in)
+            raised_in[...] = raised
+            in_total[...] = jnp.sum(raised, axis=1, keepdims=True)
+            positive = lax.broadcasted_iota(jnp.int32, shape, 1) == column
+            positive_score[...] = jnp.sum(
+                jnp.where(positive, scores_in, 0.0), axis=1, keepdims=True
+            )
+        for c in range(GATHER_CHUNKS):
+            take(0, s, c)
+            take(1, s, c)
+        when(b - 1 - s >= 0, lambda: score(b - 1 - s))
+        when(b + 1 + s <= last, lambda: score(b + 1 + s))
+
+    totals = in_total[...] + jnp.sum(hard_total[...], axis=1, keepdims=True)
     scale = sharpness_factor / totals
     for n in range(nb):
         weights = (raised_hard[n] * scale).astype(jnp.bfloat16)
@@ -409,18 +422,14 @@
         hard_parts[n] = weights
     for s in range(last):
         when(end, lambda: weight_copy(s).start())
-    shape = (rows, ng * block)
-    column = g * block + lax.rem(lax.broadcasted_iota(jnp.int32, shape, 0), block)
+    losses = jnp.log(totals) - positive_score[...]
+    for i in range(rows // block):
+        loss_out[i * block:(i + 1) * block] = jnp.sum(
+            jnp.where(diagonal, losses[i * block:(i + 1) * block], 0.0), axis=0
+        )
     positive = lax.broadcasted_iota(jnp.int32, shape, 1) == column
-    losses = jnp.log(totals) - jnp.sum(
-        jnp.where(positive, scores_in, 0.0), axis=1, keepdims=True
-    )
-    for i in range(rows // block):
-        loss_out[i:i + 1, :] = jnp.sum(
-            jnp.where(diagonal, losses[i * block:(i + 1) * block], 0.0), axis=0, keepdims=True
-        )
     grad_in[...] = (
-        raised_in * scale - jnp.where(positive, sharpness_factor, 0.0)
+        raised_in[...] * scale - jnp.where(positive, sharpness_factor, 0.0)
     ).astype(jnp.bfloat16)
 
     for n in sorted(range(nb), key=lambda n: -abs(2 * n - last)):
@@ -440,7 +449,6 @@
     for k in range(1, ng):
         back_copy(k).start()
 
-    tile = min(512, width)
     for j in range(0, width, tile):
         query_dir[:, j:j + tile] = dot(
             grad_in[...], group[:, :, j:j + tile].reshape(ng * block, tile), 1, 0
@@ -463,9 +471,9 @@
 
         def act():
             reduce(way, s, c).wait_recv()
-            own = hard_sums[target, piece(c), :].astype(jnp.float32)
-            hard_sums[target, piece(c), :] = (
-                own + landing[s, piece(c), :].astype(jnp.float32)
+            own = hard_sums[target, piece(c, SUM_CHUNKS), :].astype(jnp.float32)
+            hard_sums[target, piece(c, SUM_CHUNKS), :] = (
+                own + landing[s, piece(c, SUM_CHUNKS), :].astype(jnp.float32)
             ).astype(jnp.bfloat16)
             reduce(way, s, c).start()
 
@@ -481,7 +489,7 @@
                 own + dot(guest_hard[s], guest[:, cols], 0, 0)
             ).astype(jnp.bfloat16)
         if s < last - 1:
-            for c in range(CHUNKS):
+            for c in range(SUM_CHUNKS):
                 when(b == 1, lambda: reduce(0, s, c).start())
                 when(b == last - 1, lambda: reduce(1, s, c).start())
 
@@ -493,7 +501,7 @@
 
     when(host, serve)
     for s in range(last - 1):
-        for c in range(CHUNKS):
+        for c in range(SUM_CHUNKS):
             add_and_pass(0, s, c)
             add_and_pass(1, s, c)
     for k in range(1, ng):
@@ -507,14 +515,14 @@
 
     left_at = jnp.minimum(last - b, last - 2)
     right_at = jnp.minimum(b, last - 2)
-    for c in range(CHUNKS):
+    for c in range(SUM_CHUNKS):
         for way in (0, 1):
             for s in range(last - 1):
                 target = s if way else last - s
                 when(b == target, lambda: reduce(way, s, c).wait_recv())
 
         def finish(i, _):
-            at = pl.ds(pl.multiple_of(c * part + i * ROWS, ROWS), ROWS)
+            at = pl.ds(pl.multiple_of(c * (block // SUM_CHUNKS) + i * ROWS, ROWS), ROWS)
             direction = finish_passages(at)
             direction += jnp.where(b > 1, from_left[left_at, at, :].astype(jnp.float32), 0.0)
             direction += jnp.where(b < last - 1, from_right[right_at, at, :].astype(jnp.float32), 0.0)
@@ -524,16 +532,17 @@
             passage_out[at, :] = (norm * (direction - unit * inner)).astype(jnp.bfloat16)
             return _
 
-        lax.fori_loop(0, part // ROWS, finish, 0)
+        lax.fori_loop(0, block // SUM_CHUNKS // ROWS, finish, 0)
 
     for s in range(last):
-        for c in range(CHUNKS):
+        for c in range(GATHER_CHUNKS):
             when((b < last) & (b >= s), lambda: gather(0, b - s, s, c).wait_send())
             when((b > 0) & (b + s <= last), lambda: gather(1, b + s, s, c).wait_send())
-            if s < last - 1:
-                when((b > 0) & (b < last - s), lambda: reduce(0, s, c).wait_send())
-                when((b < last) & (b > s), lambda: reduce(1, s, c).wait_send())
         when(end, lambda: weight_copy(s).wait_send())
+    for s in range(last - 1):
+        for c in range(SUM_CHUNKS):
+            when((b > 0) & (b < last - s), lambda: reduce(0, s, c).wait_send())
+            when((b < last) & (b > s), lambda: reduce(1, s, c).wait_send())
     for c in range(2):
         when(end, lambda: guest_copy(c).wait_send())
     for k in range(1, ng):
@@ -548,15 +557,15 @@
     half, wide = jnp.bfloat16, jnp.float32
     vmem = pl.BlockSpec(memory_space=pltpu.VMEM)
     far = pl.BlockSpec(memory_space=pl.ANY)
-    line_sems = pltpu.SemaphoreType.DMA((2, nb - 1, CHUNKS))
-    sum_sems = pltpu.SemaphoreType.DMA((2, nb - 2, CHUNKS))
+    line_sems = pltpu.SemaphoreType.DMA((2, nb - 1, GATHER_CHUNKS))
+    sum_sems = pltpu.SemaphoreType.DMA((2, nb - 2, SUM_CHUNKS))
     pair_sems = pltpu.SemaphoreType.DMA((2,))
     weight_sems = pltpu.SemaphoreType.DMA((nb - 1,))
     group_sems = pltpu.SemaphoreType.DMA((ng,))
     loss, query_grad, passage_grad = pl.pallas_call(
         functools.partial(fused_kernel, nb, ng),
         out_shape=(
-            jax.ShapeDtypeStruct((rows // block, block), wide),
+            jax.ShapeDtypeStruct((rows,), wide),
             jax.ShapeDtypeStruct((rows, width), half),
             jax.ShapeDtypeStruct((block, width), half),
         ),
@@ -581,6 +590,12 @@
             pltpu.VMEM((nb, rows, block), half),
             pltpu.VMEM((rows, width), half),
             pltpu.VMEM((nb - 1, rows, block), half),
+            pltpu.VMEM((hard_owners.shape[1], rows, 1), wide),
+            pltpu.VMEM((nb, rows, block), wide),
+            pltpu.VMEM((rows, block), wide),
+            pltpu.VMEM((rows, ng * block), wide),
+            pltpu.VMEM((rows, 1), wide),
+            pltpu.VMEM((rows, 1), wide),
             pair_sems, pair_sems, pair_sems, weight_sems, weight_sems,
             line_sems, line_sems, group_sems, group_sems,
             sum_sems, sum_sems, group_sems, group_sems,
@@ -594,7 +609,7 @@
             transcendentals=rows * (nb + ng) * block,
         ),
     )(queries, passages, hard_owners.T)
-    return (loss.reshape(-1), query_grad, passage_grad)
+    return (loss, query_grad, passage_grad)
 
 
 def local(queries, passages, hard_owners):

time: 74.5 us -> 73.6 us (0.988)
  Pallas kernels: 69.2 us -> 68.4 us
    pallas_call x1, Pallas kernels: 69.2 us -> 68.4 us  [local_fused(): pl.pallas_call(functools.partial(fused_kernel, nb, ng), out_shape=(jax.Sh...]
where the time goes in v4:
time: 73.6 us; the launch traced here: 73.4 us
  Pallas kernels  68.4 us (93%)
  local copies, waits for them, and re-layouts  4.38 us (6%)
    pallas_call x1, Pallas kernels, local_fused(): pl.pallas_call(functools.partial(fused_kernel, nb, ng), out_shape=(jax.Sh...  68.4 us
    unnamed x7, local copies, waits for them, and re-layouts  4.38 us

profile of v4, /device:TPU:8, one launch (start us, length us, event | category | flops | bytes accessed | tf_op | source)
XLA Modules:
  0.0 73.4 jit_solution(745656265869157523)
XLA Ops:
  0.6 68.4 %shard_map.58 = (f32[256]{0:T(256)}, bf16[256,2048]{1,0:T(8,128)(2,1)}, bf16[128,2048]{1,0:T(8,128)(2,1)}) custom-call(bf16[256,2048]{1,0:T(8,128)(2,1)} %queries_far.1, bf16[128,2048]{1,0:T(8,128)(2,1)} %passages_far.1, s32[2,256]{1,0:T(2,128)} %bitcast.1), custom_call_target="tpu_custom_call" | custom-call | flops 3221225472 | bytes 3145728 | tf_op jit(solution)/shard_map/pallas_call | solution.py:565
  69.0 0.0 copy-start.1
  69.0 0.7 copy-done.1
  69.7 0.6 copy.9
  70.2 0.0 copy-start
  70.2 2.4 %copy.10 = bf16[256,2048]{1,0:T(8,128)(2,1)} copy(bf16[256,2048]{1,0:T(8,128)(2,1)} %get-tuple-element.7) | data formatting | bytes 2097152
  72.6 0.0 copy-done
  72.6 0.8 %copy.11 = bf16[128,2048]{1,0:T(8,128)(2,1)} copy(bf16[128,2048]{1,0:T(8,128)(2,1)S(1)} %copy-done) | data formatting | bytes 1048576
Async XLA Ops:
  69.0 0.7 copy-start.1
  70.2 2.4 %copy-start = (bf16[128,2048]{1,0:T(8,128)(2,1)S(1)}, bf16[128,2048]{1,0:T(8,128)(2,1)}, u32[]{:S(2)}) copy-start(bf16[128,2048]{1,0:T(8,128)(2,1)} %get-tuple-element.8) | copy-start | bytes 1572868

commit v5 on v4

--- a/solution.py
+++ b/solution.py
@@ -212,8 +212,7 @@
     )
 
 
-GATHER_CHUNKS = 2
-SUM_CHUNKS = 2
+PIECES = 3
 ROWS = 32
 MESH = pl.DeviceIdType.MESH
 
@@ -234,9 +233,9 @@
     queries, passages, line, group, query_half, query_norm, passage_norm,
     grad_in, grad_hard, query_dir,
     hard_sums, from_left, from_right, in_sums, from_group,
-    hard_parts, guest, guest_hard,
+    hard_parts, guest, guest_hard, share_out, share_in,
     names, raised_hard, hard_total, raised_in, in_total, positive_score,
-    load_sems, guest_send, guest_recv, weight_send, weight_recv,
+    load_sems, guest_send, guest_recv, weight_send, weight_recv, share_send, share_recv,
     gather_send, gather_recv, group_send, group_recv,
     reduce_send, reduce_recv, back_send, back_recv,
 ):
@@ -250,8 +249,9 @@
     def when(condition, act):
         pl.when(condition)(act)
 
-    def piece(c, count):
-        return pl.ds(c * (block // count), block // count)
+    low, near = width // 8 * 3, width // 8 * 5
+    columns = (pl.ds(0, low), pl.ds(low, near - low), pl.ds(near, width - near))
+    halves = (pl.ds(0, near), pl.ds(near, width - near))
 
     def along(src, dst, send, recv, step):
         return pltpu.make_async_remote_copy(
@@ -260,7 +260,7 @@
         )
 
     def gather(way, owner, s, c):
-        ref = line.at[owner, piece(c, GATHER_CHUNKS)]
+        ref = line.at[owner, :, halves[c]]
         return along(ref, ref, gather_send.at[way, s, c], gather_recv.at[way, s, c], 1 - 2 * way)
 
     def group_copy(src, dst, send, recv, k):
@@ -273,16 +273,23 @@
         target = s if way else last - s
         landing = from_right if way else from_left
         return along(
-            hard_sums.at[target, piece(c, SUM_CHUNKS)], landing.at[s, piece(c, SUM_CHUNKS)],
+            hard_sums.at[target, :, columns[c]], landing.at[s, :, columns[c]],
             reduce_send.at[way, s, c], reduce_recv.at[way, s, c], 1 - 2 * way,
         )
 
     inward = jnp.where(b == 0, 1, -1)
 
     def guest_copy(c):
-        half = pl.ds(c * (rows // 2), rows // 2)
         return along(
-            query_half.at[half], guest.at[half], guest_send.at[c], guest_recv.at[c], inward
+            query_half.at[:, columns[c]], guest.at[:, columns[c]],
+            guest_send.at[c], guest_recv.at[c], inward,
+        )
+
+    outward = jnp.where((b == 1) | (b == last), -1, 1)
+
+    def share_copy(s):
+        return along(
+            share_out.at[s], share_in.at[s], share_send.at[s], share_recv.at[s], outward
         )
 
     def weight_copy(s):
@@ -326,9 +333,10 @@
     pl.semaphore_wait(
         barrier, ng - 1 + (b > 0).astype(jnp.int32) + (b < last).astype(jnp.int32)
     )
-    for c in range(GATHER_CHUNKS):
-        when(b < last, lambda: gather(0, b, 0, c).start())
-        when(b > 0, lambda: gather(1, b, 0, c).start())
+    when(b < last, lambda: gather(0, b, 0, 0).start())
+    when(b > 0, lambda: gather(1, b, 0, 0).start())
+    when(b < last - 1, lambda: gather(0, b, 0, 1).start())
+    when(b > 1, lambda: gather(1, b, 0, 1).start())
     for k in range(1, ng):
         group_copy(group.at[g], group.at[g], group_send, group_recv, k).start()
 
@@ -342,8 +350,7 @@
 
     load_queries.wait()
     lax.fori_loop(0, rows // ROWS, norm_queries, 0)
-    for c in range(2):
-        when(end, lambda: guest_copy(c).start())
+    when(end, lambda: guest_copy(2).start())
 
     def take(way, s, c):
         owner = b + 1 + s if way else b - 1 - s
@@ -354,9 +361,12 @@
         def arrive():
             gather(way, owner, s, c).wait_recv()
             if s + 1 < last:
-                when(b > 0 if way else b < last, pass_on)
-
-        when(owner <= last if way else owner >= 0, arrive)
+                when(b > c if way else b < last - c, pass_on)
+
+        here = owner <= last if way else owner >= 0
+        if c:
+            here &= b > 0 if way else b < last
+        when(here, arrive)
 
     square = (block, block)
     diagonal = lax.broadcasted_iota(jnp.int32, square, 0) == lax.broadcasted_iota(
@@ -377,15 +387,48 @@
     for k in range(owners.shape[0]):
         names[k] = upright(owners[k:k + 1, :].astype(jnp.float32))
 
+    def named(n):
+        return functools.reduce(
+            jnp.logical_or,
+            [names[k] == n.astype(jnp.float32) for k in range(owners.shape[0])],
+        )
+
     def score(n):
         raised = jnp.exp(sharpness_factor * dot(query_half[...], line[n], 1, 1))
-        named = functools.reduce(
-            jnp.logical_or,
-            [names[k] == n.astype(jnp.float32) for k in range(owners.shape[0])],
-        )
-        raised = jnp.where(named, raised, 0.0)
+        raised = jnp.where(named(n), raised, 0.0)
         raised_hard[n] = raised
         hard_total[...] += raised
+
+    def score_near(n):
+        raised_hard[n] = sharpness_factor * dot(
+            query_half[:, halves[0]], line[n, :, halves[0]], 1, 1
+        )
+
+    def score_rest(s):
+        n = jnp.where(b == 0, 1 + s, last - 1 - s)
+        share_copy(s).wait_recv()
+        raised = jnp.exp(raised_hard[n] + share_in[s].astype(jnp.float32))
+        raised = jnp.where(named(n), raised, 0.0)
+        raised_hard[n] = raised
+        hard_total[...] += raised
+
+    def share(s):
+        n = jnp.where(b == 1, 1 + s, last - 1 - s)
+        share_out[s] = (
+            sharpness_factor * dot(guest[:, halves[1]], line[n, :, halves[1]], 1, 1)
+        ).astype(jnp.bfloat16)
+        share_copy(s).start()
+
+    def share_early():
+        guest_copy(2).wait_recv()
+        for s in range(last - 1):
+            share(s)
+
+    def share_late():
+        share(last - 1)
+        for s in range(last):
+            when(b == last - 1, lambda: gather(0, last - 1 - s, s, 1).start())
+            when(b == 1, lambda: gather(1, 1 + s, s, 1).start())
 
     hard_total[...] = jnp.zeros_like(hard_total)
     score(b)
@@ -408,11 +451,20 @@
             positive_score[...] = jnp.sum(
                 jnp.where(positive, scores_in, 0.0), axis=1, keepdims=True
             )
-        for c in range(GATHER_CHUNKS):
+        for c in range(2):
             take(0, s, c)
             take(1, s, c)
-        when(b - 1 - s >= 0, lambda: score(b - 1 - s))
-        when(b + 1 + s <= last, lambda: score(b + 1 + s))
+            if s == last - 2:
+                when(host, share_late if c else share_early)
+        left, right = b - 1 - s, b + 1 + s
+        when((left >= 0) & (b < last), lambda: score(left))
+        when((right <= last) & (b > 0), lambda: score(right))
+        when((left >= 0) & (b == last), lambda: score_near(left))
+        when((right <= last) & (b == 0), lambda: score_near(right))
+        if s == min(1, last - 1):
+            when(end, lambda: guest_copy(1).start())
+    for s in range(last):
+        when(end, lambda: score_rest(s))
 
     totals = in_total[...] + jnp.sum(hard_total[...], axis=1, keepdims=True)
     scale = sharpness_factor / totals
@@ -422,6 +474,7 @@
         hard_parts[n] = weights
     for s in range(last):
         when(end, lambda: weight_copy(s).start())
+    when(end, lambda: guest_copy(0).start())
     losses = jnp.log(totals) - positive_score[...]
     for i in range(rows // block):
         loss_out[i * block:(i + 1) * block] = jnp.sum(
@@ -449,6 +502,40 @@
     for k in range(1, ng):
         back_copy(k).start()
 
+    def add_and_pass(way, s, c):
+        target = s if way else last - s
+        landing = from_right if way else from_left
+
+        def act():
+            reduce(way, s, c).wait_recv()
+            own = hard_sums[target, :, columns[c]].astype(jnp.float32)
+            hard_sums[target, :, columns[c]] = (
+                own + landing[s, :, columns[c]].astype(jnp.float32)
+            ).astype(jnp.bfloat16)
+            reduce(way, s, c).start()
+
+        when((b < last - 1) & (b > target) if way else (b > 1) & (b < target), act)
+
+    def serve(c):
+        guest_copy(c).wait_recv() if c < 2 else None
+        for s in range(last):
+            target = jnp.where(b == 1, last - s, s)
+            if c == 2:
+                weight_copy(s).wait_recv()
+            own = hard_sums[target, :, columns[c]].astype(jnp.float32)
+            hard_sums[target, :, columns[c]] = (
+                own + dot(guest_hard[s], guest[:, columns[c]], 0, 0)
+            ).astype(jnp.bfloat16)
+            if s < last - 1:
+                when(b == 1, lambda: reduce(0, s, c).start())
+                when(b == last - 1, lambda: reduce(1, s, c).start())
+
+    when(host, lambda: serve(2))
+    when(host, lambda: serve(1))
+    for s in range(last):
+        when(b == last, lambda: gather(0, last - 1 - s, s, 1).wait_recv())
+        when(b == 0, lambda: gather(1, 1 + s, s, 1).wait_recv())
+
     for j in range(0, width, tile):
         query_dir[:, j:j + tile] = dot(
             grad_in[...], group[:, :, j:j + tile].reshape(ng * block, tile), 1, 0
@@ -465,43 +552,10 @@
 
     lax.fori_loop(0, rows // ROWS, finish_queries, 0)
 
-    def add_and_pass(way, s, c):
-        target = s if way else last - s
-        landing = from_right if way else from_left
-
-        def act():
-            reduce(way, s, c).wait_recv()
-            own = hard_sums[target, piece(c, SUM_CHUNKS), :].astype(jnp.float32)
-            hard_sums[target, piece(c, SUM_CHUNKS), :] = (
-                own + landing[s, piece(c, SUM_CHUNKS), :].astype(jnp.float32)
-            ).astype(jnp.bfloat16)
-            reduce(way, s, c).start()
-
-        when((b < last - 1) & (b > target) if way else (b > 1) & (b < target), act)
-
-    def add_guest(s):
-        target = jnp.where(b == 1, last - s, s)
-        weight_copy(s).wait_recv()
-        for j in range(0, width, tile):
-            cols = pl.ds(j, tile)
-            own = hard_sums[target, :, cols].astype(jnp.float32)
-            hard_sums[target, :, cols] = (
-                own + dot(guest_hard[s], guest[:, cols], 0, 0)
-            ).astype(jnp.bfloat16)
-        if s < last - 1:
-            for c in range(SUM_CHUNKS):
-                when(b == 1, lambda: reduce(0, s, c).start())
-                when(b == last - 1, lambda: reduce(1, s, c).start())
-
-    def serve():
-        for c in range(2):
-            guest_copy(c).wait_recv()
-        for s in range(last):
-            add_guest(s)
-
-    when(host, serve)
-    for s in range(last - 1):
-        for c in range(SUM_CHUNKS):
+    for c in (2, 1, 0):
+        if c == 1:
+            when(host, lambda: serve(0))
+        for s in range(last - 1):
             add_and_pass(0, s, c)
             add_and_pass(1, s, c)
     for k in range(1, ng):
@@ -515,35 +569,36 @@
 
     left_at = jnp.minimum(last - b, last - 2)
     right_at = jnp.minimum(b, last - 2)
-    for c in range(SUM_CHUNKS):
+    for c in range(PIECES):
         for way in (0, 1):
             for s in range(last - 1):
                 target = s if way else last - s
                 when(b == target, lambda: reduce(way, s, c).wait_recv())
 
-        def finish(i, _):
-            at = pl.ds(pl.multiple_of(c * (block // SUM_CHUNKS) + i * ROWS, ROWS), ROWS)
-            direction = finish_passages(at)
-            direction += jnp.where(b > 1, from_left[left_at, at, :].astype(jnp.float32), 0.0)
-            direction += jnp.where(b < last - 1, from_right[right_at, at, :].astype(jnp.float32), 0.0)
-            norm = passage_norm[at, :]
-            unit = passages[at, :].astype(jnp.float32) * norm
-            inner = jnp.sum(unit * direction, axis=1, keepdims=True)
-            passage_out[at, :] = (norm * (direction - unit * inner)).astype(jnp.bfloat16)
-            return _
-
-        lax.fori_loop(0, block // SUM_CHUNKS // ROWS, finish, 0)
+    def finish(i, _):
+        at = pl.ds(pl.multiple_of(i * ROWS, ROWS), ROWS)
+        direction = finish_passages(at)
+        direction += jnp.where(b > 1, from_left[left_at, at, :].astype(jnp.float32), 0.0)
+        direction += jnp.where(b < last - 1, from_right[right_at, at, :].astype(jnp.float32), 0.0)
+        norm = passage_norm[at, :]
+        unit = passages[at, :].astype(jnp.float32) * norm
+        inner = jnp.sum(unit * direction, axis=1, keepdims=True)
+        passage_out[at, :] = (norm * (direction - unit * inner)).astype(jnp.bfloat16)
+        return _
+
+    lax.fori_loop(0, block // ROWS, finish, 0)
 
     for s in range(last):
-        for c in range(GATHER_CHUNKS):
+        for c in range(2):
             when((b < last) & (b >= s), lambda: gather(0, b - s, s, c).wait_send())
             when((b > 0) & (b + s <= last), lambda: gather(1, b + s, s, c).wait_send())
         when(end, lambda: weight_copy(s).wait_send())
+        when(host, lambda: share_copy(s).wait_send())
     for s in range(last - 1):
-        for c in range(SUM_CHUNKS):
+        for c in range(PIECES):
             when((b > 0) & (b < last - s), lambda: reduce(0, s, c).wait_send())
             when((b < last) & (b > s), lambda: reduce(1, s, c).wait_send())
-    for c in range(2):
+    for c in range(PIECES):
         when(end, lambda: guest_copy(c).wait_send())
     for k in range(1, ng):
         group_copy(group.at[g], group.at[g], group_send, group_recv, k).wait_send()
@@ -557,9 +612,10 @@
     half, wide = jnp.bfloat16, jnp.float32
     vmem = pl.BlockSpec(memory_space=pltpu.VMEM)
     far = pl.BlockSpec(memory_space=pl.ANY)
-    line_sems = pltpu.SemaphoreType.DMA((2, nb - 1, GATHER_CHUNKS))
-    sum_sems = pltpu.SemaphoreType.DMA((2, nb - 2, SUM_CHUNKS))
+    line_sems = pltpu.SemaphoreType.DMA((2, nb - 1, 2))
+    sum_sems = pltpu.SemaphoreType.DMA((2, nb - 2, PIECES))
     pair_sems = pltpu.SemaphoreType.DMA((2,))
+    guest_sems = pltpu.SemaphoreType.DMA((PIECES,))
     weight_sems = pltpu.SemaphoreType.DMA((nb - 1,))
     group_sems = pltpu.SemaphoreType.DMA((ng,))
     loss, query_grad, passage_grad = pl.pallas_call(
@@ -590,13 +646,15 @@
             pltpu.VMEM((nb, rows, block), half),
             pltpu.VMEM((rows, width), half),
             pltpu.VMEM((nb - 1, rows, block), half),
+            pltpu.VMEM((nb - 1, rows, block), half),
+            pltpu.VMEM((nb - 1, rows, block), half),
             pltpu.VMEM((hard_owners.shape[1], rows, 1), wide),
             pltpu.VMEM((nb, rows, block), wide),
             pltpu.VMEM((rows, block), wide),
             pltpu.VMEM((rows, ng * block), wide),
             pltpu.VMEM((rows, 1), wide),
             pltpu.VMEM((rows, 1), wide),
-            pair_sems, pair_sems, pair_sems, weight_sems, weight_sems,
+            pair_sems, guest_sems, guest_sems, weight_sems, weight_sems, weight_sems, weight_sems,
             line_sems, line_sems, group_sems, group_sems,
             sum_sems, sum_sems, group_sems, group_sems,
         ],
@@ -614,7 +672,7 @@
 
 def local(queries, passages, hard_owners):
     nb = lax.axis_size("batch")
-    if 4 <= nb <= 8 and 1 < lax.axis_size("grp") <= 8:
+    if queries.shape[1] % 1024 == 0 and 4 <= nb <= 8 and 1 < lax.axis_size("grp") <= 8:
         return local_fused(queries, passages, hard_owners)
     if nb <= 8:
         return local_dense(queries, passages, hard_owners)

time: 73.6 us -> 73.9 us (level)
  the two profiles are of different devices: /device:TPU:8 before, /device:TPU:0 now
where the time goes in v5:
time: 73.9 us; the launch traced here: 73.7 us
  Pallas kernels  68.7 us (93%)
  local copies, waits for them, and re-layouts  4.38 us (6%)
    pallas_call x1, Pallas kernels, local_fused(): pl.pallas_call(functools.partial(fused_kernel, nb, ng), out_shape=(jax.Sh...  68.7 us
    unnamed x7, local copies, waits for them, and re-layouts  4.38 us

profile of v5, /device:TPU:0, one launch (start us, length us, event | category | flops | bytes accessed | tf_op | source)
XLA Modules:
  0.0 73.7 jit_solution(6433898369206131873)
XLA Ops:
  0.6 68.7 %shard_map.58 = (f32[256]{0:T(256)}, bf16[256,2048]{1,0:T(8,128)(2,1)}, bf16[128,2048]{1,0:T(8,128)(2,1)}) custom-call(bf16[256,2048]{1,0:T(8,128)(2,1)} %queries_far.1, bf16[128,2048]{1,0:T(8,128)(2,1)} %passages_far.1, s32[2,256]{1,0:T(2,128)} %bitcast.1), custom_call_target="tpu_custom_call" | custom-call | flops 3221225472 | bytes 3145728 | tf_op jit(solution)/shard_map/pallas_call | solution.py:621
  69.3 0.0 copy-start.1
  69.3 0.7 copy-done.1
  70.0 0.6 copy.9
  70.5 0.0 copy-start
  70.5 2.4 %copy.10 = bf16[256,2048]{1,0:T(8,128)(2,1)} copy(bf16[256,2048]{1,0:T(8,128)(2,1)} %get-tuple-element.7) | data formatting | bytes 2097152
  72.9 0.0 copy-done
  72.9 0.8 %copy.11 = bf16[128,2048]{1,0:T(8,128)(2,1)} copy(bf16[128,2048]{1,0:T(8,128)(2,1)S(1)} %copy-done) | data formatting | bytes 1048576
Async XLA Ops:
  69.3 0.7 copy-start.1
  70.5 2.4 %copy-start = (bf16[128,2048]{1,0:T(8,128)(2,1)S(1)}, bf16[128,2048]{1,0:T(8,128)(2,1)}, u32[]{:S(2)}) copy-start(bf16[128,2048]{1,0:T(8,128)(2,1)} %get-tuple-element.8) | copy-start | bytes 1572868

commit v6 on v5

--- a/solution.py
+++ b/solution.py
@@ -249,7 +249,7 @@
     def when(condition, act):
         pl.when(condition)(act)
 
-    low, near = width // 8 * 3, width // 8 * 5
+    low, near = width // 8 * 2, width // 8 * 4
     columns = (pl.ds(0, low), pl.ds(low, near - low), pl.ds(near, width - near))
     halves = (pl.ds(0, near), pl.ds(near, width - near))
 

time: 73.9 us -> 72.7 us (0.984)
  Pallas kernels: 68.7 us -> 67.5 us
    pallas_call x1, Pallas kernels: 68.7 us -> 67.5 us  [local_fused(): pl.pallas_call(functools.partial(fused_kernel, nb, ng), out_shape=(jax.Sh...]
where the time goes in v6:
time: 72.7 us; the launch traced here: 72.5 us
  Pallas kernels  67.5 us (93%)
  local copies, waits for them, and re-layouts  4.38 us (6%)
    pallas_call x1, Pallas kernels, local_fused(): pl.pallas_call(functools.partial(fused_kernel, nb, ng), out_shape=(jax.Sh...  67.5 us
    unnamed x7, local copies, waits for them, and re-layouts  4.38 us

profile of v6, /device:TPU:0, one launch (start us, length us, event | category | flops | bytes accessed | tf_op | source)
XLA Modules:
  0.0 72.5 jit_solution(5188022974553301117)
XLA Ops:
  0.6 67.5 %shard_map.58 = (f32[256]{0:T(256)}, bf16[256,2048]{1,0:T(8,128)(2,1)}, bf16[128,2048]{1,0:T(8,128)(2,1)}) custom-call(bf16[256,2048]{1,0:T(8,128)(2,1)} %queries_far.1, bf16[128,2048]{1,0:T(8,128)(2,1)} %passages_far.1, s32[2,256]{1,0:T(2,128)} %bitcast.1), custom_call_target="tpu_custom_call" | custom-call | flops 3221225472 | bytes 3145728 | tf_op jit(solution)/shard_map/pallas_call | solution.py:621
  68.1 0.0 copy-start.1
  68.1 0.7 copy-done.1
  68.8 0.6 copy.9
  69.3 0.0 copy-start
  69.3 2.4 %copy.10 = bf16[256,2048]{1,0:T(8,128)(2,1)} copy(bf16[256,2048]{1,0:T(8,128)(2,1)} %get-tuple-element.7) | data formatting | bytes 2097152
  71.7 0.0 copy-done
  71.7 0.8 %copy.11 = bf16[128,2048]{1,0:T(8,128)(2,1)} copy(bf16[128,2048]{1,0:T(8,128)(2,1)S(1)} %copy-done) | data formatting | bytes 1048576
Async XLA Ops:
  68.1 0.7 copy-start.1
  69.3 2.4 %copy-start = (bf16[128,2048]{1,0:T(8,128)(2,1)S(1)}, bf16[128,2048]{1,0:T(8,128)(2,1)}, u32[]{:S(2)}) copy-start(bf16[128,2048]{1,0:T(8,128)(2,1)} %get-tuple-element.8) | copy-start | bytes 1572868
